TPU v7x, 256 devices: a whole 4x4x8 slice. The times are simulated.
256 devices in a mesh: blk: 32 (over z, x_hi, core), outer: 8 (over x_lo, y).
Axes of the slice: x: 4 (x_hi: 2, x_lo: 2; x = x_hi * 2 + x_lo), y: 4, z: 8, core: 2. Of those that a mesh axis runs over, the one named last changes fastest.
Arguments:
- queries: float32 [16384, 1024], P('blk')
- passages: float32 [16384, 1024], P(('outer', 'blk'))
- positive_id: int32 [16384], P('blk'), may hold values from 0 to 16383, as said below
Outputs:
- question_derivative_matrix: float32 [16384, 1024], P('blk')
- grad_passages: float32 [16384, 1024], P(('outer', 'blk'))
- loss: float32 [], replicated
Inputs may be any that keep to these rules, and one draw needn't show every extreme that they name: `positive_id`: a permutation: every passage is the positive of exactly one query.
All inputs are finite; a program needn't handle non-finite values.
Results may differ from a plain program's by a relative error of at most 0.007.
Values may be sent and summed in bfloat16 or wider, within the bound.
A program may use at most 64 MiB of HBM per device.

v0:
```python
import jax
import jax.numpy as jnp
from jax import lax
from jax.sharding import PartitionSpec as P

inverse_sharpness = 125.0
norm_epsilon = 1e-06


def shifted(value, axis, steps):
    count = lax.axis_size(axis)
    pairs = [(source, (source + steps) % count) for source in range(count)]
    return lax.ppermute(value, axis, pairs)


def combined_all(value, axis, combine):
    everything = jax.tree.map(lambda part: lax.all_gather(part, axis), value)
    initial = jax.tree.map(lambda part: part[0], everything)

    def turn(k, so_far):
        return combine(so_far, jax.tree.map(lambda part: part[k], everything))

    return lax.fori_loop(1, lax.axis_size(axis), turn, initial)


def normalize(values):
    squares = jnp.sum(values * values, axis=1, keepdims=True)
    inverse = lax.rsqrt(squares + norm_epsilon)
    return (values * inverse, inverse)


def chain_through_rescaling(unit, inverse, upstream):
    along = jnp.sum(unit * upstream, axis=1, keepdims=True)
    return inverse * (upstream - unit * along)


def combine_stats(left_pair, right_pair):
    top = jnp.maximum(left_pair[0], right_pair[0])
    total = left_pair[1] * jnp.exp(left_pair[0] - top) + right_pair[1] * jnp.exp(
        right_pair[0] - top
    )
    return (top, total)


def score_tile(tile_span, question_objective_term):
    return inverse_sharpness * jnp.einsum(
        "pd,qd->pq", tile_span, question_objective_term, preferred_element_type=jnp.float32
    )


def positive_mask(positive_id, column_start, count):
    columns = column_start + lax.iota(jnp.int32, count)
    return (positive_id[None, :] == columns[:, None]).astype(jnp.float32)


def pair_weights(cosine_logit_matrix, row_lse, col_lse, mask):
    mixed = (
        0.5
        * (
            jnp.exp(cosine_logit_matrix - row_lse[None, :])
            + jnp.exp(cosine_logit_matrix - col_lse[:, None])
        )
        - mask
    )
    return mixed.astype(jnp.bfloat16)


def per_device(queries, passages, positive_id):
    blk_count = lax.axis_size("blk")
    outer_count = lax.axis_size("outer")
    blk_index = lax.axis_index("blk")
    outer_index = lax.axis_index("outer")
    block_rows = passages.shape[0]
    query_rows = queries.shape[0]
    super_cols = block_rows * blk_count
    column_base = outer_index * super_cols
    question_direction_entry, question_inverse_length = normalize(queries)
    passage_unit, passage_inverse = normalize(passages)
    question_objective_term = question_direction_entry.astype(jnp.bfloat16)
    passage_half = passage_unit.astype(jnp.bfloat16)

    def first_turn(turn, carried):
        tile_span, row_top, row_total, col_top, col_total, positive_sum = carried
        owner = (blk_index - turn) % blk_count
        cosine_logit_matrix = score_tile(tile_span, question_objective_term)
        mask = positive_mask(positive_id, column_base + owner * block_rows, block_rows)
        tile_top = jnp.max(cosine_logit_matrix, axis=1)
        tile_total = jnp.sum(jnp.exp(cosine_logit_matrix - tile_top[:, None]), axis=1)
        col_top = lax.dynamic_update_slice(col_top, tile_top[None, :], (owner, jnp.int32(0)))
        col_total = lax.dynamic_update_slice(col_total, tile_total[None, :], (owner, jnp.int32(0)))
        new_top = jnp.maximum(row_top, jnp.max(cosine_logit_matrix, axis=0))
        row_total = row_total * jnp.exp(row_top - new_top) + jnp.sum(
            jnp.exp(cosine_logit_matrix - new_top[None, :]), axis=0
        )
        positive_sum = positive_sum + jnp.sum(cosine_logit_matrix * mask)
        tile_span = shifted(tile_span, "blk", 1)
        return (tile_span, new_top, row_total, col_top, col_total, positive_sum)

    start = (
        passage_half,
        jnp.full((query_rows,), -jnp.inf, jnp.float32),
        jnp.zeros((query_rows,), jnp.float32),
        jnp.zeros((blk_count, block_rows), jnp.float32),
        jnp.zeros((blk_count, block_rows), jnp.float32),
        jnp.zeros((), jnp.float32),
    )
    carried = lax.fori_loop(0, blk_count, first_turn, start)
    row_top, row_total, col_top, col_total, positive_sum = (
        carried[1],
        carried[2],
        carried[3],
        carried[4],
        carried[5],
    )
    col_top, col_total = combined_all((col_top, col_total), "blk", combine_stats)
    row_top, row_total = combined_all((row_top, row_total), "outer", combine_stats)
    col_lse = col_top + jnp.log(col_total)
    row_lse = row_top + jnp.log(row_total)
    own_cols = lax.dynamic_index_in_dim(col_lse, blk_index, 0, keepdims=False)
    local_loss = jnp.sum(row_lse) / outer_count + jnp.sum(own_cols) - 2.0 * positive_sum
    total_loss = lax.psum(local_loss, ("blk", "outer"))
    loss = total_loss / (2.0 * super_cols * outer_count)

    def second_turn(turn, carried):
        tile_span, interim_accumulation, question_derivative = carried
        owner = (blk_index - turn) % blk_count
        cosine_logit_matrix = score_tile(tile_span, question_objective_term)
        mask = positive_mask(positive_id, column_base + owner * block_rows, block_rows)
        block_lse = lax.dynamic_index_in_dim(col_lse, owner, 0, keepdims=False)
        probability_matrix = pair_weights(cosine_logit_matrix, row_lse, block_lse, mask)
        question_derivative = question_derivative + jnp.einsum(
            "pq,pd->qd", probability_matrix, tile_span, preferred_element_type=jnp.float32
        )
        interim_accumulation = interim_accumulation + inverse_sharpness * jnp.einsum(
            "pq,qd->pd",
            probability_matrix,
            question_objective_term,
            preferred_element_type=jnp.float32,
        )
        tile_span = shifted(tile_span, "blk", 1)
        interim_accumulation = shifted(interim_accumulation, "blk", 1)
        return (tile_span, interim_accumulation, question_derivative)

    start = (
        passage_half,
        jnp.zeros(passages.shape, jnp.float32),
        jnp.zeros(queries.shape, jnp.float32),
    )
    carried = lax.fori_loop(0, blk_count, second_turn, start)
    passage_grad, question_derivative = (carried[1], carried[2])
    question_derivative = lax.psum(inverse_sharpness * question_derivative, "outer")
    question_derivative_matrix = chain_through_rescaling(
        question_direction_entry, question_inverse_length, question_derivative
    )
    grad_passages = chain_through_rescaling(passage_unit, passage_inverse, passage_grad)
    return (question_derivative_matrix, grad_passages, loss)


def solution(mesh):
    placed = (P("blk", None), P(("outer", "blk"), None), P("blk"))
    return jax.shard_map(
        per_device,
        mesh=mesh,
        in_specs=placed,
        out_specs=(P("blk", None), P(("outer", "blk"), None), P()),
        check_vma=False,
    )
```

profile of v0, /device:TPU:1, one launch (start us, length us, event | category | flops | bytes accessed | tf_op | source)
XLA Modules:
  0.0 930.5 jit_solution(15712127246028049509)
XLA Ops:
  12.2 255.9 %while.82 = (s32[]{:T(128)}, bf16[64,1024]{1,0:T(8,128)(2,1)S(1)}, f32[512]{0:T(512)S(1)}, f32[512]{0:T(512)S(1)}, f32[32,64]{1,0:T(8,128)S(1)}, /*index=5*/f32[...) while((s32[]{:T(128)}, bf16[64,1024]{1,0:T(8,128)(2,1)S(1)}, ...), condition=%wide.region_8.9_spmd.clone, body=%wide.region_2.8_spmd.clone.sunk | while | flops 67439040 | bytes 2259607 | solution.py:107
  43.4 6.1 collective-permute-done
  59.6 6.1 collective-permute-done
  67.7 6.1 collective-permute-done
  75.8 6.1 collective-permute-done
  83.9 6.1 collective-permute-done
  92.0 6.1 collective-permute-done
  100.1 6.1 collective-permute-done
  108.2 6.1 collective-permute-done
  124.4 6.1 collective-permute-done
  132.5 6.1 collective-permute-done
  140.6 6.1 collective-permute-done
  148.7 6.1 collective-permute-done
  156.8 6.1 collective-permute-done
  164.9 6.1 collective-permute-done
  173.0 6.1 collective-permute-done
  189.1 6.1 collective-permute-done
  197.3 6.1 collective-permute-done
  205.3 6.1 collective-permute-done
  213.4 6.1 collective-permute-done
  221.5 6.1 collective-permute-done
  229.6 6.1 collective-permute-done
  237.7 6.1 collective-permute-done
  253.9 6.1 collective-permute-done
  262.0 6.1 collective-permute-done
  268.1 19.6 %all-gather.4 = f32[8,1,512]{2,1,0:T(1,128)S(1)} all-gather(f32[1,1,512]{2,1,0:T(1,128)S(1)} %bitcast.68), channel_id=2, replica_groups=mesh['blk'=32,'outer'=8] {'outer'}, dimensions={0}, use_global_device_ids=true | all-gather | bytes 18432 | tf_op jit(solution)/shard_map/all_gather | solution.py:17
  287.7 19.0 %all-gather.5 = f32[8,1,512]{2,1,0:T(1,128)S(1)} all-gather(f32[1,1,512]{2,1,0:T(1,128)S(1)} %bitcast.74), channel_id=3, replica_groups=mesh['blk'=32,'outer'=8] {'outer'}, dimensions={0}, use_global_device_ids=true | all-gather | bytes 18432 | tf_op jit(solution)/shard_map/all_gather | solution.py:17
  307.2 53.4 %all-gather.3 = f32[1024,64]{1,0:T(8,128)S(1)} all-gather(f32[32,64]{1,0:T(8,128)S(1)} %get-tuple-element.787), channel_id=5, replica_groups=mesh['blk'=32,'outer'=8] {'blk'}, dimensions={0}, use_global_device_ids=true | all-gather | bytes 270336 | tf_op jit(solution)/shard_map/all_gather | solution.py:17
  360.6 41.2 %all-gather.2 = f32[1024,64]{1,0:T(8,128)S(1)} all-gather(f32[32,64]{1,0:T(8,128)S(1)} %get-tuple-element.786), channel_id=4, replica_groups=mesh['blk'=32,'outer'=8] {'blk'}, dimensions={0}, use_global_device_ids=true | all-gather | bytes 270336 | tf_op jit(solution)/shard_map/all_gather | solution.py:17
  402.7 24.1 %while.81 = (s32[]{:T(128)}, f32[32,64]{1,0:T(8,128)S(1)}, f32[32,64]{1,0:T(8,128)S(1)}, f32[32,32,64]{2,1,0:T(8,128)}, f32[32,32,64]{2,1,0:T(8,128)}, /*index=5*/s32[]{:T(128)}, s32[]{:T(128)}, s32[]{:T(128)}) while((s32[]{:T(128)}, f32[32,64]{1,0:T(8,128)S(1)}, f32[32,64]{1,0:T(8,128)S(1)}, f32[32,32,64]{2,1,0:T(8,128)}, ...), condition=%wide.region_10.11_spmd, body=%wide.region_9.10_spmd.sunk | while | flops 12293 | bytes 49275 | solution.py:23
  428.0 399.2 %while.83 = (s32[]{:T(128)}, bf16[64,1024]{1,0:T(8,128)(2,1)}, f32[64,1024]{1,0:T(8,128)S(1)}, f32[512,1024]{1,0:T(8,128)S(1)}, bf16[512,1024]{1,0:T(8,128)(2,1)...) while((s32[]{:T(128)}, bf16[64,1024]{1,0:T(8,128)(2,1)}, ...), condition=%wide.region_14.15_spmd.clone, body=%wide.region_13.14_spmd.clone.sunk | while | flops 202801232 | bytes 9377470 | solution.py:149
  831.4 85.5 %psum.15 = f32[]{:T(128)} all-reduce(f32[]{:T(128)S(6)} %sub.202), channel_id=1, replica_groups=mesh['blk'=32,'outer'=8] {'blk','outer'}, use_global_device_ids=true, to_apply=%region_20.21 | all-reduce | flops 1 | bytes 8 | tf_op jit(solution)/shard_map/psum | solution.py:121
  (808 shorter events, 527.7 us)
Async XLA Ops:
  7.2 911.4 %all-reduce.2.cloned.1.call-start = ((), (), s32[]{:S(2)}) async-start(), calls=%async_computation | async-start | bytes 4194304 | tf_op jit(solution)/shard_map/psum | solution.py:151
  474.1 9.6 %collective-permute-start.2 = (f32[64,1024]{1,0:T(8,128)}, f32[64,1024]{1,0:T(8,128)S(1)}, u32[]{:S(2)}, u32[]{:S(2)}) collective-permute-start(f32[64,1024]{1,0:T(8,128)} %fusion.37), channel_id=1, source_target_pairs={{0,8},{8,16},{16,24},{24,32},{32,40},{40,48},{48,56},{56,64},{64,7... | collective-permute-start | bytes 786440 | tf_op jit(solution)/shard_map/while/body/eval_jaxpr/ppermute | solution.py:13
  484.6 9.4 %collective-permute-start.1 = (bf16[64,1024]{1,0:T(8,128)(2,1)S(1)}, bf16[64,1024]{1,0:T(8,128)(2,1)}, u32[]{:S(2)}, u32[]{:S(2)}) collective-permute-start(bf16[64,1024]{1,0:T(8,128)(2,1)S(1)} %copy.58), channel_id=1, source_target_pairs={{0,8},{8,16},{16,24},{24,32},{32,40},{40,48},{48,56},{56,64},{64,7... | collective-permute-start | bytes 393224 | tf_op jit(solution)/shard_map/while/body/eval_jaxpr/ppermute | solution.py:13
  486.8 9.6 %collective-permute-start.2 = (f32[64,1024]{1,0:T(8,128)}, f32[64,1024]{1,0:T(8,128)S(1)}, u32[]{:S(2)}, u32[]{:S(2)}) collective-permute-start(f32[64,1024]{1,0:T(8,128)} %fusion.37), channel_id=1, source_target_pairs={{0,8},{8,16},{16,24},{24,32},{32,40},{40,48},{48,56},{56,64},{64,7... | collective-permute-start | bytes 786440 | tf_op jit(solution)/shard_map/while/body/eval_jaxpr/ppermute | solution.py:13
  499.5 9.6 %collective-permute-start.2 = (f32[64,1024]{1,0:T(8,128)}, f32[64,1024]{1,0:T(8,128)S(1)}, u32[]{:S(2)}, u32[]{:S(2)}) collective-permute-start(f32[64,1024]{1,0:T(8,128)} %fusion.37), channel_id=1, source_target_pairs={{0,8},{8,16},{16,24},{24,32},{32,40},{40,48},{48,56},{56,64},{64,7... | collective-permute-start | bytes 786440 | tf_op jit(solution)/shard_map/while/body/eval_jaxpr/ppermute | solution.py:13
  512.2 9.6 %collective-permute-start.2 = (f32[64,1024]{1,0:T(8,128)}, f32[64,1024]{1,0:T(8,128)S(1)}, u32[]{:S(2)}, u32[]{:S(2)}) collective-permute-start(f32[64,1024]{1,0:T(8,128)} %fusion.37), channel_id=1, source_target_pairs={{0,8},{8,16},{16,24},{24,32},{32,40},{40,48},{48,56},{56,64},{64,7... | collective-permute-start | bytes 786440 | tf_op jit(solution)/shard_map/while/body/eval_jaxpr/ppermute | solution.py:13
  525.0 9.6 %collective-permute-start.2 = (f32[64,1024]{1,0:T(8,128)}, f32[64,1024]{1,0:T(8,128)S(1)}, u32[]{:S(2)}, u32[]{:S(2)}) collective-permute-start(f32[64,1024]{1,0:T(8,128)} %fusion.37), channel_id=1, source_target_pairs={{0,8},{8,16},{16,24},{24,32},{32,40},{40,48},{48,56},{56,64},{64,7... | collective-permute-start | bytes 786440 | tf_op jit(solution)/shard_map/while/body/eval_jaxpr/ppermute | solution.py:13
  537.7 9.6 %collective-permute-start.2 = (f32[64,1024]{1,0:T(8,128)}, f32[64,1024]{1,0:T(8,128)S(1)}, u32[]{:S(2)}, u32[]{:S(2)}) collective-permute-start(f32[64,1024]{1,0:T(8,128)} %fusion.37), channel_id=1, source_target_pairs={{0,8},{8,16},{16,24},{24,32},{32,40},{40,48},{48,56},{56,64},{64,7... | collective-permute-start | bytes 786440 | tf_op jit(solution)/shard_map/while/body/eval_jaxpr/ppermute | solution.py:13
  550.4 9.6 %collective-permute-start.2 = (f32[64,1024]{1,0:T(8,128)}, f32[64,1024]{1,0:T(8,128)S(1)}, u32[]{:S(2)}, u32[]{:S(2)}) collective-permute-start(f32[64,1024]{1,0:T(8,128)} %fusion.37), channel_id=1, source_target_pairs={{0,8},{8,16},{16,24},{24,32},{32,40},{40,48},{48,56},{56,64},{64,7... | collective-permute-start | bytes 786440 | tf_op jit(solution)/shard_map/while/body/eval_jaxpr/ppermute | solution.py:13
  563.1 9.6 %collective-permute-start.2 = (f32[64,1024]{1,0:T(8,128)}, f32[64,1024]{1,0:T(8,128)S(1)}, u32[]{:S(2)}, u32[]{:S(2)}) collective-permute-start(f32[64,1024]{1,0:T(8,128)} %fusion.37), channel_id=1, source_target_pairs={{0,8},{8,16},{16,24},{24,32},{32,40},{40,48},{48,56},{56,64},{64,7... | collective-permute-start | bytes 786440 | tf_op jit(solution)/shard_map/while/body/eval_jaxpr/ppermute | solution.py:13
  575.8 9.6 %collective-permute-start.2 = (f32[64,1024]{1,0:T(8,128)}, f32[64,1024]{1,0:T(8,128)S(1)}, u32[]{:S(2)}, u32[]{:S(2)}) collective-permute-start(f32[64,1024]{1,0:T(8,128)} %fusion.37), channel_id=1, source_target_pairs={{0,8},{8,16},{16,24},{24,32},{32,40},{40,48},{48,56},{56,64},{64,7... | collective-permute-start | bytes 786440 | tf_op jit(solution)/shard_map/while/body/eval_jaxpr/ppermute | solution.py:13
  588.5 9.6 %collective-permute-start.2 = (f32[64,1024]{1,0:T(8,128)}, f32[64,1024]{1,0:T(8,128)S(1)}, u32[]{:S(2)}, u32[]{:S(2)}) collective-permute-start(f32[64,1024]{1,0:T(8,128)} %fusion.37), channel_id=1, source_target_pairs={{0,8},{8,16},{16,24},{24,32},{32,40},{40,48},{48,56},{56,64},{64,7... | collective-permute-start | bytes 786440 | tf_op jit(solution)/shard_map/while/body/eval_jaxpr/ppermute | solution.py:13
  601.2 9.6 %collective-permute-start.2 = (f32[64,1024]{1,0:T(8,128)}, f32[64,1024]{1,0:T(8,128)S(1)}, u32[]{:S(2)}, u32[]{:S(2)}) collective-permute-start(f32[64,1024]{1,0:T(8,128)} %fusion.37), channel_id=1, source_target_pairs={{0,8},{8,16},{16,24},{24,32},{32,40},{40,48},{48,56},{56,64},{64,7... | collective-permute-start | bytes 786440 | tf_op jit(solution)/shard_map/while/body/eval_jaxpr/ppermute | solution.py:13
  614.0 9.6 %collective-permute-start.2 = (f32[64,1024]{1,0:T(8,128)}, f32[64,1024]{1,0:T(8,128)S(1)}, u32[]{:S(2)}, u32[]{:S(2)}) collective-permute-start(f32[64,1024]{1,0:T(8,128)} %fusion.37), channel_id=1, source_target_pairs={{0,8},{8,16},{16,24},{24,32},{32,40},{40,48},{48,56},{56,64},{64,7... | collective-permute-start | bytes 786440 | tf_op jit(solution)/shard_map/while/body/eval_jaxpr/ppermute | solution.py:13
  626.7 9.6 %collective-permute-start.2 = (f32[64,1024]{1,0:T(8,128)}, f32[64,1024]{1,0:T(8,128)S(1)}, u32[]{:S(2)}, u32[]{:S(2)}) collective-permute-start(f32[64,1024]{1,0:T(8,128)} %fusion.37), channel_id=1, source_target_pairs={{0,8},{8,16},{16,24},{24,32},{32,40},{40,48},{48,56},{56,64},{64,7... | collective-permute-start | bytes 786440 | tf_op jit(solution)/shard_map/while/body/eval_jaxpr/ppermute | solution.py:13
  637.2 9.4 %collective-permute-start.1 = (bf16[64,1024]{1,0:T(8,128)(2,1)S(1)}, bf16[64,1024]{1,0:T(8,128)(2,1)}, u32[]{:S(2)}, u32[]{:S(2)}) collective-permute-start(bf16[64,1024]{1,0:T(8,128)(2,1)S(1)} %copy.58), channel_id=1, source_target_pairs={{0,8},{8,16},{16,24},{24,32},{32,40},{40,48},{48,56},{56,64},{64,7... | collective-permute-start | bytes 393224 | tf_op jit(solution)/shard_map/while/body/eval_jaxpr/ppermute | solution.py:13
  639.4 9.6 %collective-permute-start.2 = (f32[64,1024]{1,0:T(8,128)}, f32[64,1024]{1,0:T(8,128)S(1)}, u32[]{:S(2)}, u32[]{:S(2)}) collective-permute-start(f32[64,1024]{1,0:T(8,128)} %fusion.37), channel_id=1, source_target_pairs={{0,8},{8,16},{16,24},{24,32},{32,40},{40,48},{48,56},{56,64},{64,7... | collective-permute-start | bytes 786440 | tf_op jit(solution)/shard_map/while/body/eval_jaxpr/ppermute | solution.py:13
  652.1 9.6 %collective-permute-start.2 = (f32[64,1024]{1,0:T(8,128)}, f32[64,1024]{1,0:T(8,128)S(1)}, u32[]{:S(2)}, u32[]{:S(2)}) collective-permute-start(f32[64,1024]{1,0:T(8,128)} %fusion.37), channel_id=1, source_target_pairs={{0,8},{8,16},{16,24},{24,32},{32,40},{40,48},{48,56},{56,64},{64,7... | collective-permute-start | bytes 786440 | tf_op jit(solution)/shard_map/while/body/eval_jaxpr/ppermute | solution.py:13
  664.8 9.6 %collective-permute-start.2 = (f32[64,1024]{1,0:T(8,128)}, f32[64,1024]{1,0:T(8,128)S(1)}, u32[]{:S(2)}, u32[]{:S(2)}) collective-permute-start(f32[64,1024]{1,0:T(8,128)} %fusion.37), channel_id=1, source_target_pairs={{0,8},{8,16},{16,24},{24,32},{32,40},{40,48},{48,56},{56,64},{64,7... | collective-permute-start | bytes 786440 | tf_op jit(solution)/shard_map/while/body/eval_jaxpr/ppermute | solution.py:13
  677.6 9.6 %collective-permute-start.2 = (f32[64,1024]{1,0:T(8,128)}, f32[64,1024]{1,0:T(8,128)S(1)}, u32[]{:S(2)}, u32[]{:S(2)}) collective-permute-start(f32[64,1024]{1,0:T(8,128)} %fusion.37), channel_id=1, source_target_pairs={{0,8},{8,16},{16,24},{24,32},{32,40},{40,48},{48,56},{56,64},{64,7... | collective-permute-start | bytes 786440 | tf_op jit(solution)/shard_map/while/body/eval_jaxpr/ppermute | solution.py:13
  690.3 9.6 %collective-permute-start.2 = (f32[64,1024]{1,0:T(8,128)}, f32[64,1024]{1,0:T(8,128)S(1)}, u32[]{:S(2)}, u32[]{:S(2)}) collective-permute-start(f32[64,1024]{1,0:T(8,128)} %fusion.37), channel_id=1, source_target_pairs={{0,8},{8,16},{16,24},{24,32},{32,40},{40,48},{48,56},{56,64},{64,7... | collective-permute-start | bytes 786440 | tf_op jit(solution)/shard_map/while/body/eval_jaxpr/ppermute | solution.py:13
  703.0 9.6 %collective-permute-start.2 = (f32[64,1024]{1,0:T(8,128)}, f32[64,1024]{1,0:T(8,128)S(1)}, u32[]{:S(2)}, u32[]{:S(2)}) collective-permute-start(f32[64,1024]{1,0:T(8,128)} %fusion.37), channel_id=1, source_target_pairs={{0,8},{8,16},{16,24},{24,32},{32,40},{40,48},{48,56},{56,64},{64,7... | collective-permute-start | bytes 786440 | tf_op jit(solution)/shard_map/while/body/eval_jaxpr/ppermute | solution.py:13
  715.7 9.6 %collective-permute-start.2 = (f32[64,1024]{1,0:T(8,128)}, f32[64,1024]{1,0:T(8,128)S(1)}, u32[]{:S(2)}, u32[]{:S(2)}) collective-permute-start(f32[64,1024]{1,0:T(8,128)} %fusion.37), channel_id=1, source_target_pairs={{0,8},{8,16},{16,24},{24,32},{32,40},{40,48},{48,56},{56,64},{64,7... | collective-permute-start | bytes 786440 | tf_op jit(solution)/shard_map/while/body/eval_jaxpr/ppermute | solution.py:13
  728.5 9.6 %collective-permute-start.2 = (f32[64,1024]{1,0:T(8,128)}, f32[64,1024]{1,0:T(8,128)S(1)}, u32[]{:S(2)}, u32[]{:S(2)}) collective-permute-start(f32[64,1024]{1,0:T(8,128)} %fusion.37), channel_id=1, source_target_pairs={{0,8},{8,16},{16,24},{24,32},{32,40},{40,48},{48,56},{56,64},{64,7... | collective-permute-start | bytes 786440 | tf_op jit(solution)/shard_map/while/body/eval_jaxpr/ppermute | solution.py:13
  739.0 9.4 %collective-permute-start.1 = (bf16[64,1024]{1,0:T(8,128)(2,1)S(1)}, bf16[64,1024]{1,0:T(8,128)(2,1)}, u32[]{:S(2)}, u32[]{:S(2)}) collective-permute-start(bf16[64,1024]{1,0:T(8,128)(2,1)S(1)} %copy.58), channel_id=1, source_target_pairs={{0,8},{8,16},{16,24},{24,32},{32,40},{40,48},{48,56},{56,64},{64,7... | collective-permute-start | bytes 393224 | tf_op jit(solution)/shard_map/while/body/eval_jaxpr/ppermute | solution.py:13
  741.2 9.6 %collective-permute-start.2 = (f32[64,1024]{1,0:T(8,128)}, f32[64,1024]{1,0:T(8,128)S(1)}, u32[]{:S(2)}, u32[]{:S(2)}) collective-permute-start(f32[64,1024]{1,0:T(8,128)} %fusion.37), channel_id=1, source_target_pairs={{0,8},{8,16},{16,24},{24,32},{32,40},{40,48},{48,56},{56,64},{64,7... | collective-permute-start | bytes 786440 | tf_op jit(solution)/shard_map/while/body/eval_jaxpr/ppermute | solution.py:13
  753.9 9.6 %collective-permute-start.2 = (f32[64,1024]{1,0:T(8,128)}, f32[64,1024]{1,0:T(8,128)S(1)}, u32[]{:S(2)}, u32[]{:S(2)}) collective-permute-start(f32[64,1024]{1,0:T(8,128)} %fusion.37), channel_id=1, source_target_pairs={{0,8},{8,16},{16,24},{24,32},{32,40},{40,48},{48,56},{56,64},{64,7... | collective-permute-start | bytes 786440 | tf_op jit(solution)/shard_map/while/body/eval_jaxpr/ppermute | solution.py:13
  766.7 9.6 %collective-permute-start.2 = (f32[64,1024]{1,0:T(8,128)}, f32[64,1024]{1,0:T(8,128)S(1)}, u32[]{:S(2)}, u32[]{:S(2)}) collective-permute-start(f32[64,1024]{1,0:T(8,128)} %fusion.37), channel_id=1, source_target_pairs={{0,8},{8,16},{16,24},{24,32},{32,40},{40,48},{48,56},{56,64},{64,7... | collective-permute-start | bytes 786440 | tf_op jit(solution)/shard_map/while/body/eval_jaxpr/ppermute | solution.py:13
  779.4 9.6 %collective-permute-start.2 = (f32[64,1024]{1,0:T(8,128)}, f32[64,1024]{1,0:T(8,128)S(1)}, u32[]{:S(2)}, u32[]{:S(2)}) collective-permute-start(f32[64,1024]{1,0:T(8,128)} %fusion.37), channel_id=1, source_target_pairs={{0,8},{8,16},{16,24},{24,32},{32,40},{40,48},{48,56},{56,64},{64,7... | collective-permute-start | bytes 786440 | tf_op jit(solution)/shard_map/while/body/eval_jaxpr/ppermute | solution.py:13
  792.1 9.6 %collective-permute-start.2 = (f32[64,1024]{1,0:T(8,128)}, f32[64,1024]{1,0:T(8,128)S(1)}, u32[]{:S(2)}, u32[]{:S(2)}) collective-permute-start(f32[64,1024]{1,0:T(8,128)} %fusion.37), channel_id=1, source_target_pairs={{0,8},{8,16},{16,24},{24,32},{32,40},{40,48},{48,56},{56,64},{64,7... | collective-permute-start | bytes 786440 | tf_op jit(solution)/shard_map/while/body/eval_jaxpr/ppermute | solution.py:13
  804.8 9.6 %collective-permute-start.2 = (f32[64,1024]{1,0:T(8,128)}, f32[64,1024]{1,0:T(8,128)S(1)}, u32[]{:S(2)}, u32[]{:S(2)}) collective-permute-start(f32[64,1024]{1,0:T(8,128)} %fusion.37), channel_id=1, source_target_pairs={{0,8},{8,16},{16,24},{24,32},{32,40},{40,48},{48,56},{56,64},{64,7... | collective-permute-start | bytes 786440 | tf_op jit(solution)/shard_map/while/body/eval_jaxpr/ppermute | solution.py:13
  817.6 9.6 %collective-permute-start.2 = (f32[64,1024]{1,0:T(8,128)}, f32[64,1024]{1,0:T(8,128)S(1)}, u32[]{:S(2)}, u32[]{:S(2)}) collective-permute-start(f32[64,1024]{1,0:T(8,128)} %fusion.37), channel_id=1, source_target_pairs={{0,8},{8,16},{16,24},{24,32},{32,40},{40,48},{48,56},{56,64},{64,7... | collective-permute-start | bytes 786440 | tf_op jit(solution)/shard_map/while/body/eval_jaxpr/ppermute | solution.py:13
  (107 other events, 900.2 us)
Sparse Core Ops, SparseCore 0:
  828.8 88.7 all-reduce.1
where the time goes:
time: 941 us; the launch traced here: 930 us
  waiting for transfers between devices  419 us (45%)
  blocking collectives  219 us (23%)
  matrix products  114 us (12%)
  other arithmetic  59 us (6%)
  local copies, waits for them, and re-layouts  55.6 us (6%)
  starting transfers between devices  26 us (3%)
  loops' own time  21.3 us (2%)
  between operations  17.2 us (2%)
    ppermute x96, waiting for transfers between devices, shifted(): return lax.ppermute(value, axis, pairs)  419 us
    all_gather x4, blocking collectives, combined_all(): everything = jax.tree.map(lambda part: lax.all_gather(part, axis), value)  133 us
    psum x1, blocking collectives, per_device(): total_loss = lax.psum(local_loss, ('blk', 'outer'))  85.5 us
    dot_general x32, matrix products, second_turn(): jnp.einsum('pq,pd->qd', probability_matrix, tile_span, preferred_element_...  48.8 us
    dot_general x64, matrix products, score_tile(): jnp.einsum('pd,qd->pq', tile_span, question_objective_term, preferred_ele...  32.6 us
    dot_general x32, matrix products, second_turn(): jnp.einsum('pq,qd->pd', probability_matrix, question_objective_term, pref...  32.2 us
    while x160, local copies, waits for them, and re-layouts  29.5 us
    ppermute x96, starting transfers between devices, shifted(): return lax.ppermute(value, axis, pairs)  25.9 us
  transfers between devices with their start and end apart: 97, of which 94 were waited for; matrix products, arithmetic and copies ran while one was open for 17% of the time, Pallas kernels for 0%

commit v1 on v0

v1 whole, which is shorter than its diff:
```python
import jax
import jax.numpy as jnp
from jax import lax
from jax.sharding import PartitionSpec as P

inverse_sharpness = 125.0
norm_epsilon = 1e-06


def normalize(values):
    squares = jnp.sum(values * values, axis=1, keepdims=True)
    inverse = lax.rsqrt(squares + norm_epsilon)
    return (values * inverse, inverse)


def chain_through_rescaling(unit, inverse, upstream):
    along = jnp.sum(unit * upstream, axis=1, keepdims=True)
    return inverse * (upstream - unit * along)


def per_device(queries, passages, positive_id):
    blk_count = lax.axis_size("blk")
    outer_count = lax.axis_size("outer")
    outer_index = lax.axis_index("outer")
    block_rows = passages.shape[0]
    super_cols = block_rows * blk_count
    column_base = outer_index * super_cols
    q_unit, q_inv = normalize(queries)
    p_unit, p_inv = normalize(passages)
    q_half = q_unit.astype(jnp.bfloat16)
    p_half = p_unit.astype(jnp.bfloat16)
    p_all = lax.all_gather(p_half, "blk", axis=0, tiled=True)
    scores = inverse_sharpness * jnp.einsum(
        "pd,qd->pq", p_all, q_half, preferred_element_type=jnp.float32
    )
    columns = column_base + lax.iota(jnp.int32, super_cols)
    mask = (positive_id[None, :] == columns[:, None]).astype(jnp.float32)
    col_top = jnp.max(scores, axis=1)
    col_total = jnp.sum(jnp.exp(scores - col_top[:, None]), axis=1)
    row_top = jnp.max(scores, axis=0)
    row_total = jnp.sum(jnp.exp(scores - row_top[None, :]), axis=0)
    positive = jnp.sum(scores * mask, axis=0)
    col_all = lax.all_gather(jnp.stack([col_top, col_total]), "blk")
    row_all = lax.all_gather(jnp.stack([row_top, row_total, positive]), "outer")
    col_max = jnp.max(col_all[:, 0], axis=0)
    col_lse = col_max + jnp.log(
        jnp.sum(col_all[:, 1] * jnp.exp(col_all[:, 0] - col_max[None]), axis=0)
    )
    row_max = jnp.max(row_all[:, 0], axis=0)
    row_lse = row_max + jnp.log(
        jnp.sum(row_all[:, 1] * jnp.exp(row_all[:, 0] - row_max[None]), axis=0)
    )
    positives = jnp.sum(row_all[:, 2])
    local = (jnp.sum(row_lse) - 2.0 * positives) / outer_count + jnp.sum(col_lse) / blk_count
    loss = lax.psum(local, ("blk", "outer")) / (2.0 * super_cols * outer_count)
    weights = (
        0.5 * (jnp.exp(scores - row_lse[None, :]) + jnp.exp(scores - col_lse[:, None])) - mask
    ).astype(jnp.bfloat16)
    p_part = inverse_sharpness * jnp.einsum(
        "pq,qd->pd", weights, q_half, preferred_element_type=jnp.float32
    )
    p_grad = lax.psum_scatter(p_part, "blk", scatter_dimension=0, tiled=True)
    q_part = inverse_sharpness * jnp.einsum(
        "pq,pd->qd", weights, p_all, preferred_element_type=jnp.float32
    )
    q_grad = lax.psum(q_part, "outer")
    return (
        chain_through_rescaling(q_unit, q_inv, q_grad),
        chain_through_rescaling(p_unit, p_inv, p_grad),
        loss,
    )


def solution(mesh):
    placed = (P("blk", None), P(("outer", "blk"), None), P("blk"))
    return jax.shard_map(
        per_device,
        mesh=mesh,
        in_specs=placed,
        out_specs=(P("blk", None), P(("outer", "blk"), None), P()),
        check_vma=False,
    )
```

time: 941 us -> 439 us (0.47)
  waiting for transfers between devices: 419 us -> 237 us
  matrix products: 114 us -> 16.9 us
  blocking collectives: 219 us -> 147 us
  local copies, waits for them, and re-layouts: 55.6 us -> 0.08 us
  other arithmetic: 59 us -> 15.8 us
  starting transfers between devices: 26 us -> 0.12 us
  loops' own time: 21.3 us -> 0 us
    ppermute x96 -> x0, waiting for transfers between devices: 419 us -> none  [shifted(): return lax.ppermute(value, axis, pairs)]
    reduce_scatter x0 -> x1, waiting for transfers between devices: none -> 146 us  [per_device(): p_grad = lax.psum_scatter(p_part, 'blk', scatter_dimension=0, tiled=True)]
    dot_general x128 -> x3, matrix products: 114 us -> 16.9 us  [the longest x1 7.1 us: per_device(): jnp.einsum('pq,qd->pd', weights, q_half, preferred_element_type=jnp.float32)]
    all_gather x0 -> x1, waiting for transfers between devices: none -> 90.5 us  [per_device(): p_all = lax.all_gather(p_half, 'blk', axis=0, tiled=True)]
    all_gather x4 -> x2, blocking collectives: 133 us -> 68.8 us  [the longest x1 46.9 us: per_device(): col_all = lax.all_gather(jnp.stack([col_top, col_total]), 'blk')]
    while x160 -> x0, local copies, waits for them, and re-layouts: 29.5 us -> none
    ppermute x96 -> x0, starting transfers between devices: 25.9 us -> none  [shifted(): return lax.ppermute(value, axis, pairs)]
    add x135 -> x1, other arithmetic: 25 us -> 0.01 us  [per_device(): columns = column_base + lax.iota(jnp.int32, super_cols)]
  transfers between devices with their start and end apart: 97 -> 3, of which waited for: 94 -> 2; matrix products, arithmetic and copies ran while one was open for 17% -> 3% of each run, Pallas kernels for 0% -> 0%
where the time goes in v1:
time: 439 us; the launch traced here: 435 us
  waiting for transfers between devices  237 us (54%)
  blocking collectives  147 us (33%)
  between operations  17.6 us (4%)
  matrix products  16.9 us (4%)
  other arithmetic  15.8 us (4%)
    reduce_scatter x1, waiting for transfers between devices, per_device(): p_grad = lax.psum_scatter(p_part, 'blk', scatter_dimension=0, tiled=True)  146 us
    all_gather x1, waiting for transfers between devices, per_device(): p_all = lax.all_gather(p_half, 'blk', axis=0, tiled=True)  90.5 us
    psum x1, blocking collectives, per_device(): loss = lax.psum(local, ('blk', 'outer')) / (2.0 * super_cols * outer_count)  78.4 us
    all_gather x1, blocking collectives, per_device(): col_all = lax.all_gather(jnp.stack([col_top, col_total]), 'blk')  46.9 us
    all_gather x1, blocking collectives, per_device(): row_all = lax.all_gather(jnp.stack([row_top, row_total, positive]), 'outer')  21.9 us
  transfers between devices with their start and end apart: 3, of which 2 were waited for; matrix products, arithmetic and copies ran while one was open for 3% of the time, Pallas kernels for 0%

profile of v1, /device:TPU:1, one launch (start us, length us, event | category | flops | bytes accessed | tf_op | source)
XLA Modules:
  0.0 434.6 jit_solution(15682058058161642733)
XLA Ops:
  7.2 0.0 all-gather.6.cloned.1.call-start
  7.2 1.1 multiply_reduce_fusion.3
  8.3 1.7 multiply_convert_fusion.1
  10.0 0.0 all-gather.6.cloned.1.call-update
  10.0 0.0 all-reduce.2.cloned.1.call-start
  10.1 1.8 multiply_reduce_fusion.1
  11.9 0.0 copy-start.4
  11.9 90.5 %all-gather.6.cloned.1.call-done = bf16[2048,1024]{1,0:T(8,128)(2,1)} async-done(((bf16[64,1024]{1,0:T(8,128)(2,1)}), bf16[2048,1024]{1,0:T(8,128)(2,1)}) %all-gather.6.cloned.1.call-update) | async-done | bytes 4194320 | tf_op jit(solution)/shard_map/all_gather | solution.py:32
  102.4 5.6 %fusion.12 = (f32[512]{0:T(512)S(1)}, f32[2048]{0:T(1024)S(1)}, f32[2048,512]{1,0:T(8,128)S(1)}) fusion(bf16[2048,1024]{1,0:T(8,128)(2,1)} %all-gather.6.cloned.1.call-done, f32[512,1024]{1,0:T(8,128)} %param.3, f32[512]{0:T(512)S(1)} %add_rsqrt_fusion), kind=kOutput, calls=%fused_computation.38 | convolution fusion | flops 2151675392 | bytes 10498048 | tf_op jit(solution)/shard_map/pd,qd->pq/dot_general | solution.py:33
  108.0 1.8 exponential_reduce_fusion.1
  109.8 21.9 %all-gather.2 = f32[8,3,512]{2,1,0:T(4,128)S(1)} all-gather(f32[1,3,512]{2,1,0:T(4,128)S(1)} %maximum_bitcast_fusion.1), channel_id=2, replica_groups=mesh['blk'=32,'outer'=8] {'outer'}, dimensions={0}, use_global_device_ids=true | all-gather | bytes 55296 | tf_op jit(solution)/shard_map/all_gather | solution.py:44
  131.8 0.6 fusion.16
  132.4 0.7 fusion.14
  133.1 46.9 %all-gather.3 = f32[32,2,2048]{2,1,0:T(2,128)S(1)} all-gather(f32[1,2,2048]{2,1,0:T(2,128)S(1)} %maximum_bitcast_fusion), channel_id=3, replica_groups=mesh['blk'=32,'outer'=8] {'blk'}, dimensions={0}, use_global_device_ids=true | all-gather | bytes 540672 | tf_op jit(solution)/shard_map/all_gather | solution.py:43
  180.0 0.5 fusion.15
  180.5 0.2 fusion.4
  180.7 0.6 fusion.13
  181.3 0.0 copy-done.2
  181.3 4.2 convolution_multiply_fusion.2
  185.6 0.0 all-reduce.2.cloned.1.call-update
  185.6 0.0 reduce-scatter.2.cloned.1.call-start
  185.6 0.0 copy-done
  185.6 7.1 %convolution_multiply_fusion = f32[2048,1024]{1,0:T(8,128)} fusion(f32[512,1024]{1,0:T(8,128)S(1)} %copy-done, f32[512]{0:T(512)S(1)} %add_rsqrt_fusion, f32[2048,512]{1,0:T(8,128)} %copy-done.2, f32[2048]{0:T(1024)S(1)} %get-tuple-element.11, f32[512]{0:T(512)S(1)} %get-tuple-element.13, s32[512]{0:T(512)S(1)} %copy-done.4, s32[2048]{0:T(1024)S(1)} %iota_add_fusion), kind=kOutput, calls=%fused_computation.2 | convolution fusion | flops 2159017984 | bytes 14702592 | tf_op jit(solution)/shard_map/pq,qd->pd/dot_general | solution.py:59
  192.7 0.0 reduce-scatter.2.cloned.1.call-update
  194.7 78.4 %psum.15 = f32[]{:T(128)} all-reduce(f32[]{:T(128)S(6)} %add.67), channel_id=1, replica_groups=mesh['blk'=32,'outer'=8] {'blk','outer'}, use_global_device_ids=true, to_apply=%region_18.0 | all-reduce | flops 1 | bytes 8 | tf_op jit(solution)/shard_map/psum | solution.py:55
  273.7 0.0 all-reduce.2.cloned.1.call-done
  273.7 2.2 multiply_reduce_fusion
  275.9 0.1 copy-done.1
  276.0 1.7 subtract_multiply_fusion
  277.7 146.3 %reduce-scatter.2.cloned.1.call-done = f32[64,1024]{1,0:T(8,128)} async-done(((f32[2048,1024]{1,0:T(8,128)}), f32[64,1024]{1,0:T(8,128)}) %reduce-scatter.2.cloned.1.call-update) | async-done | bytes 262160 | tf_op jit(solution)/shard_map/reduce_scatter | solution.py:62
  424.0 1.2 multiply_reduce_fusion.2
  425.1 1.8 subtract_multiply_fusion.1
  (14 shorter events, 0.1 us)
Async XLA Ops:
  7.2 95.3 %all-gather.6.cloned.1.call-start = ((), (), s32[]{:S(2)}) async-start(), calls=%async_computation.1 | async-start | bytes 4325376 | tf_op jit(solution)/shard_map/all_gather | solution.py:32
  10.0 263.7 %all-reduce.2.cloned.1.call-start = ((), (), s32[]{:S(2)}) async-start(), calls=%async_computation.2 | async-start | bytes 4194304 | tf_op jit(solution)/shard_map/psum | solution.py:66
  11.9 96.1 %copy-start.4 = (s32[512]{0:T(512)S(1)}, s32[512]{0:T(512)}, u32[]{:S(2)}) copy-start(s32[512]{0:T(512)} %param.5) | copy-start | bytes 6148
  108.0 73.4 %copy-start.2 = (f32[2048,512]{1,0:T(8,128)}, f32[2048,512]{1,0:T(8,128)S(1)}, u32[]{:S(2)}) copy-start(f32[2048,512]{1,0:T(8,128)S(1)} %get-tuple-element.21) | copy-start | bytes 12582916
  108.0 73.3 %copy-start.5 = (bf16[2048,1024]{1,0:T(8,128)(2,1)S(1)}, bf16[2048,1024]{1,0:T(8,128)(2,1)}, u32[]{:S(2)}) copy-start(bf16[2048,1024]{1,0:T(8,128)(2,1)} %all-gather.6.cloned.1.call-done) | copy-start | bytes 12582916
  181.3 4.3 copy-start
  185.6 238.4 %reduce-scatter.2.cloned.1.call-start = ((), (), s32[]{:S(2)}) async-start(), calls=%async_computation.3 | async-start | bytes 8650752 | tf_op jit(solution)/shard_map/reduce_scatter | solution.py:62
  273.7 2.2 copy-start.1
  276.0 148.0 %copy-start.3 = (f32[64,1024]{1,0:T(8,128)S(1)}, f32[64,1024]{1,0:T(8,128)}, u32[]{:S(2)}) copy-start(f32[64,1024]{1,0:T(8,128)} %param.4) | copy-start | bytes 786436
Sparse Core Ops, SparseCore 0:
  11.4 91.0 all-gather.5
  185.7 79.9 all-reduce.1
  270.1 153.8 reduce-scatter.1

commit v2 on v1

v2 whole, which is shorter than its diff:
```python
import jax
import jax.numpy as jnp
from jax import lax
from jax.experimental import pallas as pl
from jax.experimental.pallas import tpu as pltpu
from jax.sharding import PartitionSpec as P

MESH = pl.DeviceIdType.MESH
SHARP = 125.0
EPS = 1e-06
D = 1024
NQ = 512
NP = 64
NB = 32
NO = 8
NZ = 8
GROUP = 4 * NP
F32 = jnp.float32
BF16 = jnp.bfloat16
NT = (((1,), (1,)), ((), ()))
NN = (((1,), (0,)), ((), ()))
TN = (((0,), (0,)), ((), ()))


def dot(a, b, dims):
    return lax.dot_general(a, b, dims, preferred_element_type=F32)


def lse_of(parts, axis):
    top = jnp.max(parts, axis=axis, keepdims=True)
    return top + jnp.log(jnp.sum(jnp.exp(parts - top), axis=axis, keepdims=True))


def kernel(
    q_ref, p_ref, id_ref,
    qo_ref, po_ref, loss_ref,
    pall, qh, scores, weights, mine, pres, sib_out, sib_in, ring_out, ring_in,
    x_out, x_in, q_out, q_in, q_fin, q_own,
    row_part, pos_acc, col_part, col_sib, col_chip, col_all, row_all,
    sum_r, sum_r_sib, sum_r_chip, sum_r_all, sum_c_all,
    ag_ss, ag_rs, cs_ss, cs_rs, col_ss, col_rs, row_ss, row_rs,
    sib_ss, sib_rs, ring_ss, ring_rs, x_ss, x_rs, q_ss, q_rs, f_ss, f_rs,
    r1_ss, r1_rs, ra_ss, ra_rs, ca_ss, ca_rs,
):
    b = lax.axis_index("blk")
    o = lax.axis_index("outer")
    c = lax.rem(b, 2)
    xh = lax.rem(lax.div(b, 2), 2)
    z = lax.div(b, 4)
    chip = z * 2 + xh

    def blk_of(zz, xx, cc):
        return (zz * 2 + xx) * 2 + cc

    def wrap(dz):
        return lax.rem(z + dz + 16, NZ)

    def at(zz, xx, cc):
        return (blk_of(zz, xx, cc), o)

    sib = at(z, xh, 1 - c)
    x2 = at(z, 1 - xh, c)
    up = at(wrap(1), xh, c)
    down = at(wrap(-1), xh, c)

    def chip_peer(k):
        other = lax.rem(chip + k, 16)
        return other, (other * 2 + c, o)

    def outer_peer(k):
        other = lax.rem(o + k, NO)
        return other, (b, other)

    def copy(src, dst, ss, rs, dev):
        return pltpu.make_async_remote_copy(
            src_ref=src, dst_ref=dst, send_sem=ss, recv_sem=rs, device_id=dev, device_id_type=MESH
        )

    barrier = pltpu.get_barrier_semaphore()
    pl.semaphore_signal(barrier, inc=1, device_id=sib, device_id_type=MESH)

    def greet_chip(k, _):
        pl.semaphore_signal(barrier, inc=1, device_id=chip_peer(k)[1], device_id_type=MESH)
        return 0

    def greet_outer(k, _):
        pl.semaphore_signal(barrier, inc=1, device_id=outer_peer(k)[1], device_id_type=MESH)
        return 0

    lax.fori_loop(1, 16, greet_chip, 0)
    lax.fori_loop(1, NO, greet_outer, 0)

    def rows(i, n=NP):
        return pl.ds(pl.multiple_of(i * n, n), n)

    def shard(i):
        return pall.at[rows(i)]

    pv = p_ref[...]
    p_inv = lax.rsqrt(jnp.sum(pv * pv, axis=1, keepdims=True) + EPS)
    pall[rows(b), :] = (pv * p_inv).astype(BF16)
    pl.semaphore_wait(barrier, 23)

    def ag_copy(i, k, dev):
        return copy(shard(i), shard(i), ag_ss.at[k], ag_rs.at[i], dev)

    def ag_send(i, k, *devs):
        for n, dev in enumerate(devs):
            ag_copy(i, k + n, dev).start()

    def ag_wait(i):
        ag_copy(i, 0, sib).wait_recv()

    ag_send(b, 0, up, down, x2, sib)

    def norm_q(i, _):
        v = q_ref[rows(i), :]
        inv = lax.rsqrt(jnp.sum(v * v, axis=1, keepdims=True) + EPS)
        qh[rows(i), :] = (v * inv).astype(BF16)
        return 0

    lax.fori_loop(0, NQ // NP, norm_q, 0)
    pos_acc[...] = jnp.zeros_like(pos_acc)

    def own(dz, xrel):
        return blk_of(wrap(dz), xh if xrel == 0 else 1 - xh, c)

    def got(dz, xrel, k, *devs):
        i = own(dz, xrel)
        ag_wait(i)
        ag_send(i, k, *devs)

    def from_sib(dz):
        ag_wait(blk_of(wrap(dz), 0, 1 - c))
        ag_wait(blk_of(wrap(dz), 1, 1 - c))

    sign = 2 * xh - 1

    def far(xrel, k):
        s = sign if xrel == 0 else -sign
        i = blk_of(wrap(3 * s), xh if xrel == 0 else 1 - xh, c)
        ag_send(i, k, at(wrap(-s), xh, c))

    def gather_turn(t):
        if t == 0:
            got(0, 1, 4, sib)
            got(-1, 0, 5, up, x2, sib)
            got(1, 0, 8, down, x2, sib)
            from_sib(0)
        if t == 1:
            got(-1, 1, 11, sib)
            got(1, 1, 12, sib)
            got(-2, 0, 13, up, x2, sib)
            got(2, 0, 16, down, x2, sib)
            from_sib(-1)
        if t == 2:
            from_sib(1)
        if t == 3:
            got(-2, 1, 19, up, sib)
            got(2, 1, 21, down, sib)
            got(-3, 0, 23, sib)
            got(3, 0, 24, sib)
            far(0, 25)
            from_sib(-2)
        if t == 4:
            from_sib(2)
        if t == 5:
            got(-3, 1, 26, sib)
            got(3, 1, 27, sib)
            far(1, 28)
            from_sib(-3)
        if t == 6:
            got(4, 0, 29, sib)
            got(4, 1, 30, sib)
            from_sib(3)
        if t == 7:
            from_sib(4)

    base = o * (NB * NP)

    def mask_of(zz):
        cols = base + zz * GROUP + lax.broadcasted_iota(jnp.int32, (GROUP, NQ), 0)
        return cols == id_ref[...]

    def first(t, _):
        for k in range(8):
            pl.when(t == k)(lambda k=k: gather_turn(k))
        far_by = lax.div(t + 1, 2)
        zz = wrap(jnp.where(lax.rem(t, 2) == 1, -far_by, far_by))
        pg = pall[rows(zz, GROUP), :]
        s = SHARP * dot(pg, qh[...], NT)
        scores[rows(zz, GROUP), :] = s
        row_part[pl.ds(t, 1), :] = lse_of(s, 0)
        pos_acc[...] += jnp.sum(jnp.where(mask_of(zz), s, 0.0), axis=0, keepdims=True)
        st = SHARP * dot(qh[...], pg, NT)
        col_part[pl.ds(zz, 1), :] = lse_of(st, 0)
        return 0

    lax.fori_loop(0, 8, first, 0)

    sib_col = copy(col_part, col_sib, cs_ss.at[0], cs_rs.at[0], sib)
    sib_col.start()
    row_lse_part = lse_of(row_part[...], 0)
    pos_part = pos_acc[...]
    for k in range(4):
        row_all[o, k : k + 1, :] = row_lse_part[:, 128 * k : 128 * k + 128]
        row_all[o, 4 + k : 5 + k, :] = pos_part[:, 128 * k : 128 * k + 128]

    def row_copy(k):
        other, dev = outer_peer(k)
        send = copy(row_all.at[o], row_all.at[o], row_ss.at[k], row_rs.at[o], dev)
        recv = copy(row_all.at[o], row_all.at[other], row_ss.at[k], row_rs.at[other], dev)
        return send, recv

    def row_start(k, _):
        row_copy(k)[0].start()
        return 0

    lax.fori_loop(1, NO, row_start, 0)
    sib_col.wait_recv()
    a0, a1 = col_part[...], col_sib[...]
    top = jnp.maximum(a0, a1)
    col_all[chip] = top + jnp.log(jnp.exp(a0 - top) + jnp.exp(a1 - top))

    def col_copy(k):
        other, dev = chip_peer(k)
        send = copy(col_all.at[chip], col_all.at[chip], col_ss.at[k], col_rs.at[chip], dev)
        recv = copy(col_all.at[chip], col_all.at[other], col_ss.at[k], col_rs.at[other], dev)
        return send, recv

    def col_start(k, _):
        col_copy(k)[0].start()
        return 0

    lax.fori_loop(1, 16, col_start, 0)

    def row_wait(k, _):
        row_copy(k)[1].wait_recv()
        return 0

    lax.fori_loop(1, NO, row_wait, 0)
    rall = row_all[...]
    row_lse4 = lse_of(rall[:, 0:4, :], 0)[0]
    pos4 = jnp.sum(rall[:, 4:8, :], axis=0)
    row_lse = jnp.concatenate([row_lse4[k : k + 1, :] for k in range(4)], axis=1)
    sum_r[...] = jnp.broadcast_to(jnp.sum(row_lse4 - 2.0 * pos4, keepdims=True), (8, 128))
    sib_r = copy(sum_r, sum_r_sib, r1_ss.at[0], r1_rs.at[0], sib)
    sib_r.start()

    def col_wait(k, _):
        col_copy(k)[1].wait_recv()
        return 0

    lax.fori_loop(1, 16, col_wait, 0)
    col_lse = lse_of(col_all[...], 0)[0]
    col_chip[...] = col_lse
    sum_c_all[o] = jnp.broadcast_to(jnp.sum(col_lse, keepdims=True), (8, 128))

    def c_copy(k):
        other, dev = outer_peer(k)
        send = copy(sum_c_all.at[o], sum_c_all.at[o], ca_ss.at[k], ca_rs.at[o], dev)
        recv = copy(sum_c_all.at[o], sum_c_all.at[other], ca_ss.at[k], ca_rs.at[other], dev)
        return send, recv

    def sib_copy(i):
        return copy(sib_out.at[i], sib_in.at[i], sib_ss.at[i], sib_rs.at[i], sib)

    def joined(dz, xx):
        i = wrap(dz) * 2 + xx
        sib_copy(i).wait_recv()
        mine[i] = mine[i] + sib_in[i].astype(F32)

    def slot(way, d, xx):
        return way * 8 + (d - 1) * 2 + xx

    def ring_copy(way, d, xx):
        i = slot(way, d, xx)
        return copy(ring_out.at[i], ring_in.at[i], ring_ss.at[i], ring_rs.at[i], up if way == 0 else down)

    def ring_send(way, d, xx, carry):
        i = wrap(d if way == 0 else -d) * 2 + xx
        value = mine[i]
        if carry:
            ring_copy(way, d + 1, xx).wait_recv()
            value = value + ring_in[slot(way, d + 1, xx)].astype(F32)
        ring_out[slot(way, d, xx)] = value.astype(BF16)
        ring_copy(way, d, xx).start()

    def scatter_turn(t):
        if t == 1:
            joined(4, 0)
            joined(4, 1)
            ring_send(0, 4, 0, False)
            ring_send(1, 4, 1, False)
        if t == 3:
            joined(3, 1)
            joined(-3, 0)
            ring_send(0, 3, 1, False)
            ring_send(1, 3, 0, False)
            joined(3, 0)
            joined(-3, 1)
        if t == 5:
            for xx in range(2):
                joined(2, xx)
                joined(-2, xx)
        if t == 7:
            for xx in range(2):
                joined(1, xx)
                joined(-1, xx)

    def second(t, _):
        far_by = 4 - lax.div(t + 1, 2)
        zz = wrap(jnp.where(lax.rem(t, 2) == 1, far_by, -far_by))
        s = scores[rows(zz, GROUP), :]
        cl = jnp.broadcast_to(col_chip[pl.ds(zz, 1), :], (8, GROUP)).T[:, 0:1]
        w = 0.5 * (jnp.exp(s - row_lse) + jnp.exp(s - cl)) - jnp.where(mask_of(zz), 1.0, 0.0)
        w = w.astype(BF16)
        weights[rows(zz, GROUP), :] = w
        pres[...] = SHARP * dot(w, qh[...], NN)
        for xx in range(2):
            i = zz * 2 + xx
            sib_out[i] = pres[rows(xx * 2 + 1 - c), :].astype(BF16)
            sib_copy(i).start()
            mine[i] = pres[rows(xx * 2 + c), :]
        for k in (1, 3, 5, 7):
            pl.when(t == k)(lambda k=k: scatter_turn(k))
        return 0

    lax.fori_loop(0, 8, second, 0)

    def q_copy(other):
        dev = (b, other)
        send = copy(q_out.at[other], q_in.at[o], q_ss.at[other], q_rs.at[o], dev)
        recv = copy(q_out.at[other], q_in.at[other], q_ss.at[other], q_rs.at[other], dev)
        return send, recv

    def q_chunk(k, _):
        k = lax.rem(k + lax.div(o, 2), 4)
        w = weights[:, pl.ds(pl.multiple_of(k * 128, 128), 128)]
        g = dot(w, pall[...], TN)
        for h in range(2):
            other = 2 * k + h
            part = g[h * NP : (h + 1) * NP, :]

            @pl.when(other == o)
            def _():
                q_own[...] = part

            @pl.when(other != o)
            def _():
                q_out[other] = part.astype(BF16)
                q_copy(other)[0].start()

        return 0

    lax.fori_loop(0, 4, q_chunk, 0)

    def c_start(k, _):
        c_copy(k)[0].start()
        return 0

    lax.fori_loop(1, NO, c_start, 0)

    ring_send(0, 3, 0, True)
    ring_send(1, 3, 1, True)
    ring_send(0, 2, 1, True)
    ring_send(1, 2, 0, True)
    sib_r.wait_recv()
    sum_r_all[chip] = sum_r[...] + sum_r_sib[...]

    def r_copy(k):
        other, dev = chip_peer(k)
        send = copy(sum_r_all.at[chip], sum_r_all.at[chip], ra_ss.at[k], ra_rs.at[chip], dev)
        recv = copy(sum_r_all.at[chip], sum_r_all.at[other], ra_ss.at[k], ra_rs.at[other], dev)
        return send, recv

    def r_start(k, _):
        r_copy(k)[0].start()
        return 0

    lax.fori_loop(1, 16, r_start, 0)
    ring_send(0, 2, 0, True)
    ring_send(1, 2, 1, True)
    ring_send(0, 1, 1, True)
    ring_send(1, 1, 0, True)

    def q_add(k, _):
        other, _dev = outer_peer(k)
        q_copy(other)[1].wait_recv()
        q_own[...] += q_in[other].astype(F32)
        return 0

    lax.fori_loop(1, NO, q_add, 0)
    qv = q_ref[rows(o), :]
    q_inv = lax.rsqrt(jnp.sum(qv * qv, axis=1, keepdims=True) + EPS)
    qu = qv * q_inv
    qg = SHARP * q_own[...]
    q_fin[o] = (q_inv * (qg - qu * jnp.sum(qu * qg, axis=1, keepdims=True))).astype(BF16)

    def f_copy(k):
        other, dev = outer_peer(k)
        send = copy(q_fin.at[o], q_fin.at[o], f_ss.at[k], f_rs.at[o], dev)
        recv = copy(q_fin.at[o], q_fin.at[other], f_ss.at[k], f_rs.at[other], dev)
        return send, recv

    def f_start(k, _):
        f_copy(k)[0].start()
        return 0

    lax.fori_loop(1, NO, f_start, 0)

    ring_send(0, 1, 0, True)
    ring_send(1, 1, 1, True)

    def total(xx):
        i = z * 2 + xx
        for way in range(2):
            copy(
                ring_out.at[slot(way, 1, xx)], ring_in.at[slot(way, 1, xx)],
                ring_ss.at[slot(way, 1, xx)], ring_rs.at[slot(way, 1, xx)], up,
            ).wait_recv()
        return (
            mine[i]
            + ring_in[slot(0, 1, xx)].astype(F32)
            + ring_in[slot(1, 1, xx)].astype(F32)
        )

    joined(0, 0)
    joined(0, 1)
    x_out[...] = total(1 - xh).astype(BF16)
    x_copy = copy(x_out, x_in, x_ss.at[0], x_rs.at[0], x2)
    x_copy.start()
    pg_own = total(xh)

    def c_wait(k, _):
        c_copy(k)[1].wait_recv()
        return 0

    def r_wait(k, _):
        r_copy(k)[1].wait_recv()
        return 0

    lax.fori_loop(1, NO, c_wait, 0)
    lax.fori_loop(1, 16, r_wait, 0)
    loss_ref[...] = (jnp.sum(sum_r_all[...], axis=0) + jnp.sum(sum_c_all[...], axis=0)) / (
        2.0 * NB * NP * NO
    )

    qo_ref[rows(o), :] = q_fin[o].astype(F32)

    def f_wait(k, _):
        other, _dev = outer_peer(k)
        f_copy(k)[1].wait_recv()
        qo_ref[rows(other), :] = q_fin[other].astype(F32)
        return 0

    lax.fori_loop(1, NO, f_wait, 0)

    x_copy.wait_recv()
    pu = p_ref[...]
    p_inv2 = lax.rsqrt(jnp.sum(pu * pu, axis=1, keepdims=True) + EPS)
    pu = pu * p_inv2
    g = pg_own + x_in[...].astype(F32)
    po_ref[...] = p_inv2 * (g - pu * jnp.sum(pu * g, axis=1, keepdims=True))

    def ag_done(k, _):
        ag_copy(b, k, sib).wait_send()
        return 0

    lax.fori_loop(0, 31, ag_done, 0)
    sib_col.wait_send()
    sib_r.wait_send()
    x_copy.wait_send()

    def outer_done(k, _):
        row_copy(k)[0].wait_send()
        c_copy(k)[0].wait_send()
        f_copy(k)[0].wait_send()
        q_copy(outer_peer(k)[0])[0].wait_send()
        return 0

    lax.fori_loop(1, NO, outer_done, 0)

    def chip_done(k, _):
        col_copy(k)[0].wait_send()
        r_copy(k)[0].wait_send()
        return 0

    lax.fori_loop(1, 16, chip_done, 0)

    def sib_done(k, _):
        sib_copy(k).wait_send()
        return 0

    lax.fori_loop(0, 16, sib_done, 0)
    for way in range(2):
        for d in (1, 2, 3, 4):
            for xx in range(2):
                if d < 4 or xx == way:
                    ring_copy(way, d, xx).wait_send()


def per_device(queries, passages, positive_id):
    vmem = pl.BlockSpec(memory_space=pltpu.VMEM)
    dma = pltpu.SemaphoreType.DMA
    scratch = [
        pltpu.VMEM((NB * NP, D), BF16),
        pltpu.VMEM((NQ, D), BF16),
        pltpu.VMEM((NB * NP, NQ), F32),
        pltpu.VMEM((NB * NP, NQ), BF16),
        pltpu.VMEM((16, NP, D), F32),
        pltpu.VMEM((GROUP, D), F32),
        pltpu.VMEM((16, NP, D), BF16),
        pltpu.VMEM((16, NP, D), BF16),
        pltpu.VMEM((16, NP, D), BF16),
        pltpu.VMEM((16, NP, D), BF16),
        pltpu.VMEM((NP, D), BF16),
        pltpu.VMEM((NP, D), BF16),
        pltpu.VMEM((NO, NP, D), BF16),
        pltpu.VMEM((NO, NP, D), BF16),
        pltpu.VMEM((NO, NP, D), BF16),
        pltpu.VMEM((NP, D), F32),
        pltpu.VMEM((8, NQ), F32),
        pltpu.VMEM((1, NQ), F32),
        pltpu.VMEM((NZ, GROUP), F32),
        pltpu.VMEM((NZ, GROUP), F32),
        pltpu.VMEM((NZ, GROUP), F32),
        pltpu.VMEM((16, NZ, GROUP), F32),
        pltpu.VMEM((NO, 8, 128), F32),
        pltpu.VMEM((8, 128), F32),
        pltpu.VMEM((8, 128), F32),
        pltpu.VMEM((8, 128), F32),
        pltpu.VMEM((16, 8, 128), F32),
        pltpu.VMEM((NO, 8, 128), F32),
        dma((31,)), dma((NB,)),
        dma((1,)), dma((1,)),
        dma((16,)), dma((16,)),
        dma((NO,)), dma((NO,)),
        dma((16,)), dma((16,)),
        dma((16,)), dma((16,)),
        dma((1,)), dma((1,)),
        dma((NO,)), dma((NO,)),
        dma((NO,)), dma((NO,)),
        dma((1,)), dma((1,)),
        dma((16,)), dma((16,)),
        dma((NO,)), dma((NO,)),
    ]
    qd, pd, loss = pl.pallas_call(
        kernel,
        out_shape=(
            jax.ShapeDtypeStruct((NQ, D), F32),
            jax.ShapeDtypeStruct((NP, D), F32),
            jax.ShapeDtypeStruct((8, 128), F32),
        ),
        in_specs=[vmem, vmem, vmem],
        out_specs=(vmem, vmem, vmem),
        scratch_shapes=scratch,
        compiler_params=pltpu.CompilerParams(
            collective_id=0, has_side_effects=True, vmem_limit_bytes=56 * 2**20
        ),
    )(queries, passages, positive_id.reshape(1, NQ))
    return qd, pd, loss[0, 0]


def solution(mesh):
    placed = (P("blk", None), P(("outer", "blk"), None), P("blk"))
    return jax.shard_map(
        per_device,
        mesh=mesh,
        in_specs=placed,
        out_specs=(P("blk", None), P(("outer", "blk"), None), P()),
        check_vma=False,
    )
```

time: 439 us -> 102 us (0.23)
  waiting for transfers between devices: 237 us -> 0 us
  blocking collectives: 147 us -> 0 us
  Pallas kernels: 0 us -> 95.9 us
  between operations: 17.6 us -> 0.64 us
  matrix products: 16.9 us -> 0 us
  other arithmetic: 15.8 us -> 0 us
  local copies, waits for them, and re-layouts: 0.08 us -> 5.1 us
    reduce_scatter x1 -> x0, waiting for transfers between devices: 146 us -> none  [per_device(): p_grad = lax.psum_scatter(p_part, 'blk', scatter_dimension=0, tiled=True)]
    pallas_call x0 -> x1, Pallas kernels: none -> 95.9 us  [per_device(): pl.pallas_call(kernel, out_shape=(jax.ShapeDtypeStruct((NQ, D), F32), jax...]
    all_gather x1 -> x0, waiting for transfers between devices: 90.5 us -> none  [per_device(): p_all = lax.all_gather(p_half, 'blk', axis=0, tiled=True)]
    psum x1 -> x0, blocking collectives: 78.4 us -> none  [per_device(): loss = lax.psum(local, ('blk', 'outer')) / (2.0 * super_cols * outer_count)]
    all_gather x2 -> x0, blocking collectives: 68.8 us -> none  [the longest x1 46.9 us: per_device(): col_all = lax.all_gather(jnp.stack([col_top, col_total]), 'blk')]
    dot_general x3 -> x0, matrix products: 16.9 us -> none  [the longest x1 7.1 us: per_device(): jnp.einsum('pq,qd->pd', weights, q_half, preferred_element_type=jnp.float32)]
    reduce_sum x9 -> x0, other arithmetic: 9.48 us -> none  [the longest x2 3.31 us: chain_through_rescaling(): along = jnp.sum(unit * upstream, axis=1, keepdims=True)]
  transfers between devices with their start and end apart: 3 -> 0, of which waited for: 2 -> 0; matrix products, arithmetic and copies ran while one was open for 3% -> 0% of each run, Pallas kernels for 0% -> 0%
where the time goes in v2:
time: 102 us
  Pallas kernels  95.9 us (94%)
  local copies, waits for them, and re-layouts  5.1 us (5%)
    pallas_call x1, Pallas kernels, per_device(): pl.pallas_call(kernel, out_shape=(jax.ShapeDtypeStruct((NQ, D), F32), jax...  95.9 us
    unnamed x4, local copies, waits for them, and re-layouts  3.91 us

profile of v2, /device:TPU:1, one launch (start us, length us, event | category | flops | bytes accessed | tf_op | source)
XLA Modules:
  0.0 101.7 jit_solution(4355591606123293651)
XLA Ops:
  0.6 95.9 %shard_map.58 = (f32[512,1024]{1,0:T(8,128)}, f32[64,1024]{1,0:T(8,128)}, f32[8,128]{1,0:T(8,128)}) custom-call(f32[512,1024]{1,0:T(8,128)} %q_ref.1, f32[64,1024]{1,0:T(8,128)} %p_ref.1, s32[1,512]{1,0:T(1,128)} %bitcast.2), custom_call_target="tpu_custom_call" | custom-call | tf_op jit(solution)/shard_map/pallas_call | solution.py:548
  96.6 1.2 %slice.3 = f32[1,1]{1,0:T(1,128)} slice(f32[8,128]{1,0:T(8,128)} %get-tuple-element.8), slice={[0:1], [0:1]} | slice | bytes 8 | tf_op jit(solution)/shard_map/slice | solution.py:562
  97.8 0.0 copy-start
  97.8 3.2 %copy.8 = f32[512,1024]{1,0:T(8,128)} copy(f32[512,1024]{1,0:T(8,128)} %get-tuple-element.12) | data formatting | bytes 4194304
  101.0 0.0 copy-done
  101.0 0.7 copy.9
Async XLA Ops:
  97.8 3.2 %copy-start = (f32[64,1024]{1,0:T(8,128)S(1)}, f32[64,1024]{1,0:T(8,128)}, u32[]{:S(2)}) copy-start(f32[64,1024]{1,0:T(8,128)} %get-tuple-element.13) | copy-start | bytes 786436

commit v3 on v2

v3 whole, which is shorter than its diff:
```python
import jax
import jax.numpy as jnp
from jax import lax
from jax.experimental import pallas as pl
from jax.experimental.pallas import tpu as pltpu
from jax.sharding import PartitionSpec as P

MESH = pl.DeviceIdType.MESH
SHARP = 125.0
EPS = 1e-06
LN2 = 0.6931471805599453
SHARP2 = SHARP / LN2
HALF = 32
CROSS = (0,)
D = 1024
NQ = 512
NP = 64
NB = 32
NO = 8
NZ = 8
GROUP = 4 * NP
F32 = jnp.float32
BF16 = jnp.bfloat16
NT = (((1,), (1,)), ((), ()))
NN = (((1,), (0,)), ((), ()))
TN = (((0,), (0,)), ((), ()))


def dot(a, b, dims):
    return lax.dot_general(a, b, dims, preferred_element_type=F32)


def lse_of(parts, axis):
    top = jnp.max(parts, axis=axis, keepdims=True)
    return top + jnp.log(jnp.sum(jnp.exp2(parts - top), axis=axis, keepdims=True)) * (1.0 / LN2)


def kernel(
    q_any, p_any, id_any,
    q_fin, po_ref, loss_ref,
    q_ref, p_ref, id_ref, in_sem,
    pall, qh, scores, weights, mine, pres, sib_out, sib_in, ring_out, ring_in,
    x_out, x_in, q_out, q_in, q_own,
    row_part, row_wide, pos_acc, col_part, col_sib, col_wide, col_all, row_all,
    sum_r, sum_r_sib, sum_r_all, sum_c_all,
    ag_ss, ag_rs, as_ss, cs_ss, cs_rs, col_ss, col_rs, row_ss, row_rs,
    sib_ss, sib_rs, ring_ss, ring_rs, x_ss, x_rs, q_ss, q_rs, f_ss, f_rs,
    r1_ss, r1_rs, ra_ss, ra_rs, ca_ss, ca_rs,
):
    b = lax.axis_index("blk")
    o = lax.axis_index("outer")
    c = lax.rem(b, 2)
    xh = lax.rem(lax.div(b, 2), 2)
    z = lax.div(b, 4)
    chip = z * 2 + xh

    def blk_of(zz, xx, cc):
        return (zz * 2 + xx) * 2 + cc

    def wrap(dz):
        return lax.rem(z + dz + 16, NZ)

    def at(zz, xx, cc):
        return (blk_of(zz, xx, cc), o)

    sib = at(z, xh, 1 - c)
    x2 = at(z, 1 - xh, c)
    up = at(wrap(1), xh, c)
    down = at(wrap(-1), xh, c)

    def chip_peer(k):
        other = lax.rem(chip + k, 16)
        return other, (other * 2 + c, o)

    def outer_peer(k):
        other = lax.rem(o + k, NO)
        return other, (b, other)

    def copy(src, dst, ss, rs, dev):
        return pltpu.make_async_remote_copy(
            src_ref=src, dst_ref=dst, send_sem=ss, recv_sem=rs, device_id=dev, device_id_type=MESH
        )

    p_load = pltpu.make_async_copy(p_any, p_ref, in_sem.at[0])
    q_load = pltpu.make_async_copy(q_any, q_ref, in_sem.at[1])
    id_load = pltpu.make_async_copy(id_any, id_ref, in_sem.at[2])
    p_load.start()
    barrier = pltpu.get_barrier_semaphore()
    for dev in (x2, up, down, sib):
        pl.semaphore_signal(barrier, inc=1, device_id=dev, device_id_type=MESH)

    def greet_outer(k, _):
        pl.semaphore_signal(barrier, inc=1, device_id=outer_peer(k)[1], device_id_type=MESH)
        return 0

    lax.fori_loop(1, NO, greet_outer, 0)
    q_load.start()
    id_load.start()

    def rows(i, n=NP):
        return pl.ds(pl.multiple_of(i * n, n), n)

    def shard(i):
        return pall.at[rows(i)]

    p_load.wait()
    pv = p_ref[...]
    p_inv = lax.rsqrt(jnp.sum(pv * pv, axis=1, keepdims=True) + EPS)
    pall[rows(b), :] = (pv * p_inv).astype(BF16)
    pl.semaphore_wait(barrier, 4 + NO - 1)

    def piece(i, h):
        return pall.at[pl.ds(pl.multiple_of(i * NP + h * HALF, HALF), HALF)]

    def ag_copy(i, h, k, dev):
        return copy(piece(i, h), piece(i, h), ag_ss.at[k], ag_rs.at[i * 2 + h], dev)

    def as_copy(i, k):
        return copy(shard(i), shard(i), as_ss.at[k], ag_rs.at[i * 2], sib)

    sent = [0, 0]

    def pass_on(i, h, *devs):
        for dev in devs:
            ag_copy(i, h, sent[0], dev).start()
            sent[0] += 1

    def to_sib(i):
        as_copy(i, sent[1]).start()
        sent[1] += 1

    for h in range(2):
        pass_on(b, h, up, down, x2)
    to_sib(b)

    def norm_q(i, _):
        v = q_ref[rows(i), :]
        inv = lax.rsqrt(jnp.sum(v * v, axis=1, keepdims=True) + EPS)
        qh[rows(i), :] = (v * inv).astype(BF16)
        return 0

    q_load.wait()
    lax.fori_loop(0, NQ // NP, norm_q, 0)
    id_load.wait()
    pos_acc[...] = jnp.zeros_like(pos_acc)

    def own(dz, xrel):
        return blk_of(wrap(dz), xh if xrel == 0 else 1 - xh, c)

    sign = 2 * xh - 1

    def got(dz, xrel):
        sides = (dz,) if dz in (0, 4) else (-dz, dz)
        for h in range(2):
            for d in sides:
                i = own(d, xrel)
                ag_copy(i, h, 0, sib).wait_recv()
                if xrel == 0 and dz in CROSS and dz > 0:
                    pass_on(i, h, x2)
                if dz < 3 and (xrel == 0 or dz + 1 not in CROSS):
                    if d <= 0:
                        pass_on(i, h, up)
                    if d >= 0:
                        pass_on(i, h, down)
            if dz == 3 and (xrel == 0 or 4 not in CROSS):
                s = sign if xrel == 0 else -sign
                pass_on(
                    blk_of(wrap(3 * s), xh if xrel == 0 else 1 - xh, c), h, at(wrap(-s), xh, c)
                )
        for d in sides:
            to_sib(own(d, xrel))

    def from_sib(dz):
        for xx in range(2):
            as_copy(blk_of(wrap(dz), xx, 1 - c), 0).wait_recv()

    def gather_turn(t):
        if t == 0:
            got(0, 1)
            got(1, 0)
            from_sib(0)
        if t == 1:
            got(1, 1)
            got(2, 0)
            from_sib(-1)
        if t == 2:
            got(2, 1)
            from_sib(1)
        if t == 3:
            got(3, 0)
            from_sib(-2)
        if t == 4:
            got(3, 1)
            from_sib(2)
        if t == 5:
            from_sib(-3)
        if t == 6:
            got(4, 0)
            got(4, 1)
            from_sib(3)
        if t == 7:
            from_sib(4)

    base = o * (NB * NP)

    def mask_of(zz):
        cols = base + zz * GROUP + lax.broadcasted_iota(jnp.int32, (GROUP, NQ), 0)
        return cols == id_ref[...]

    def first(t, _):
        for k in range(8):
            pl.when(t == k)(lambda k=k: gather_turn(k))
        far_by = lax.div(t + 1, 2)
        zz = wrap(jnp.where(lax.rem(t, 2) == 1, -far_by, far_by))
        pg = pall[rows(zz, GROUP), :]
        s = SHARP2 * dot(pg, qh[...], NT)
        scores[rows(zz, GROUP), :] = s
        row_part[pl.ds(t, 1), :] = lse_of(s, 0)
        pos_acc[...] += jnp.sum(jnp.where(mask_of(zz), s, 0.0), axis=0, keepdims=True)
        st = SHARP2 * dot(qh[...], pg, NT)
        col_part[pl.ds(zz, 1), :] = lse_of(st, 0)
        return 0

    lax.fori_loop(0, 8, first, 0)

    sib_col = copy(col_part, col_sib, cs_ss.at[0], cs_rs.at[0], sib)
    sib_col.start()
    row_lse_part = lse_of(row_part[...], 0)
    pos_part = pos_acc[...]
    for k in range(4):
        row_all[o, k : k + 1, :] = row_lse_part[:, 128 * k : 128 * k + 128]
        row_all[o, 4 + k : 5 + k, :] = pos_part[:, 128 * k : 128 * k + 128]

    def row_copy(k):
        other, dev = outer_peer(k)
        send = copy(row_all.at[o], row_all.at[o], row_ss.at[k], row_rs.at[o], dev)
        recv = copy(row_all.at[o], row_all.at[other], row_ss.at[k], row_rs.at[other], dev)
        return send, recv

    def row_start(k, _):
        row_copy(k)[0].start()
        return 0

    lax.fori_loop(1, NO, row_start, 0)
    sib_col.wait_recv()
    a0, a1 = col_part[...], col_sib[...]
    top = jnp.maximum(a0, a1)
    col_all[chip] = top + jnp.log(jnp.exp2(a0 - top) + jnp.exp2(a1 - top)) * (1.0 / LN2)

    def col_copy(k):
        other, dev = chip_peer(k)
        send = copy(col_all.at[chip], col_all.at[chip], col_ss.at[k], col_rs.at[chip], dev)
        recv = copy(col_all.at[chip], col_all.at[other], col_ss.at[k], col_rs.at[other], dev)
        return send, recv

    def col_start(k, _):
        col_copy(k)[0].start()
        return 0

    lax.fori_loop(1, 16, col_start, 0)

    def row_wait(k, _):
        row_copy(k)[1].wait_recv()
        return 0

    lax.fori_loop(1, NO, row_wait, 0)
    rall = row_all[...]
    row_lse4 = lse_of(rall[:, 0:4, :], 0)[0]
    pos4 = jnp.sum(rall[:, 4:8, :], axis=0)
    row_wide[...] = row_lse4 + 1.0
    sum_r[...] = jnp.broadcast_to(jnp.sum(row_lse4 - 2.0 * pos4, keepdims=True), (8, 128))
    sib_r = copy(sum_r, sum_r_sib, r1_ss.at[0], r1_rs.at[0], sib)
    sib_r.start()

    def col_wait(k, _):
        col_copy(k)[1].wait_recv()
        return 0

    lax.fori_loop(1, 16, col_wait, 0)
    col_lse = lse_of(col_all[...], 0)[0]
    for k in range(NZ):
        col_wide[k * GROUP : (k + 1) * GROUP, :] = jnp.broadcast_to(
            col_lse[k : k + 1, :] + 1.0, (128, GROUP)
        ).T
    sum_c_all[o] = jnp.broadcast_to(jnp.sum(col_lse, keepdims=True), (8, 128))

    def c_copy(k):
        other, dev = outer_peer(k)
        send = copy(sum_c_all.at[o], sum_c_all.at[o], ca_ss.at[k], ca_rs.at[o], dev)
        recv = copy(sum_c_all.at[o], sum_c_all.at[other], ca_ss.at[k], ca_rs.at[other], dev)
        return send, recv

    def q_copy(other):
        dev = (b, other)
        send = copy(q_out.at[other], q_in.at[o], q_ss.at[other], q_rs.at[o], dev)
        recv = copy(q_out.at[other], q_in.at[other], q_ss.at[other], q_rs.at[other], dev)
        return send, recv

    def q_chunk(k, _):
        k = lax.rem(k + lax.div(o, 2), 4)
        lanes = pl.ds(pl.multiple_of(k * 128, 128), 128)
        rl = row_wide[pl.ds(k, 1), :]
        ids = id_ref[:, lanes] - base

        def tile(g, _):
            s = scores[rows(g, GROUP), lanes]
            cols = g * GROUP + lax.broadcasted_iota(jnp.int32, (GROUP, 128), 0)
            w = jnp.exp2(s - rl) + jnp.exp2(s - col_wide[rows(g, GROUP), :])
            weights[rows(g, GROUP), lanes] = (w - jnp.where(cols == ids, 1.0, 0.0)).astype(BF16)
            return 0

        lax.fori_loop(0, NZ, tile, 0)
        g = dot(weights[:, lanes], pall[...], TN)
        for h in range(2):
            other = 2 * k + h
            part = g[h * NP : (h + 1) * NP, :]

            @pl.when(other == o)
            def _():
                q_own[...] = part

            @pl.when(other != o)
            def _():
                q_out[other] = part.astype(BF16)
                q_copy(other)[0].start()

        return 0

    lax.fori_loop(0, 4, q_chunk, 0)

    def sib_copy(i):
        return copy(sib_out.at[i], sib_in.at[i], sib_ss.at[i], sib_rs.at[i], sib)

    def slot(way, d, xx):
        return way * 8 + (d - 1) * 2 + xx

    def ring_copy(way, d, xx, h):
        i = slot(way, d, xx)
        part = pl.ds(h * HALF, HALF)
        return copy(
            ring_out.at[i, part], ring_in.at[i, part],
            ring_ss.at[i * 2 + h], ring_rs.at[i * 2 + h], up if way == 0 else down,
        )

    def arrived(way, d, xx, h):
        ring_copy(way, d, xx, h).wait_recv()
        return ring_in[slot(way, d, xx), h * HALF : (h + 1) * HALF, :].astype(F32)

    def joined(dz, xx, h):
        i = wrap(dz) * 2 + xx
        if h == 0:
            sib_copy(i).wait_recv()
        part = slice(h * HALF, (h + 1) * HALF)
        return mine[i, part, :] + sib_in[i, part, :].astype(F32)

    def ring_send(d, xx_up, carry):
        for h in range(2):
            for way, xx in ((0, xx_up), (1, 1 - xx_up)):
                value = joined(d if way == 0 else -d, xx, h)
                if carry:
                    value = value + arrived(way, d + 1, xx, h)
                ring_out[slot(way, d, xx), h * HALF : (h + 1) * HALF, :] = value.astype(BF16)
                ring_copy(way, d, xx, h).start()

    def second(t, _):
        far_by = 4 - lax.div(t + 1, 2)
        zz = wrap(jnp.where(lax.rem(t, 2) == 1, far_by, -far_by))
        pres[...] = SHARP * dot(weights[rows(zz, GROUP), :], qh[...], NN)
        for xx in range(2):
            i = zz * 2 + xx
            sib_out[i] = pres[rows(xx * 2 + 1 - c), :].astype(BF16)
            sib_copy(i).start()
            mine[i] = pres[rows(xx * 2 + c), :]
        pl.when(t == 1)(lambda: ring_send(4, 0, False))
        pl.when(t == 3)(lambda: ring_send(3, 1, False))
        return 0

    lax.fori_loop(0, 8, second, 0)

    def c_start(k, _):
        c_copy(k)[0].start()
        return 0

    lax.fori_loop(1, NO, c_start, 0)
    ring_send(3, 0, True)
    sib_r.wait_recv()
    sum_r_all[chip] = sum_r[...] + sum_r_sib[...]

    def r_copy(k):
        other, dev = chip_peer(k)
        send = copy(sum_r_all.at[chip], sum_r_all.at[chip], ra_ss.at[k], ra_rs.at[chip], dev)
        recv = copy(sum_r_all.at[chip], sum_r_all.at[other], ra_ss.at[k], ra_rs.at[other], dev)
        return send, recv

    def r_start(k, _):
        r_copy(k)[0].start()
        return 0

    lax.fori_loop(1, 16, r_start, 0)

    def q_add(k, _):
        other, _dev = outer_peer(k)
        q_copy(other)[1].wait_recv()
        q_own[...] += q_in[other].astype(F32)
        return 0

    lax.fori_loop(1, NO, q_add, 0)
    qv = q_ref[rows(o), :]
    q_inv = lax.rsqrt(jnp.sum(qv * qv, axis=1, keepdims=True) + EPS)
    qu = qv * q_inv
    qg = SHARP * q_own[...]
    q_fin[rows(o), :] = (q_inv * (qg - qu * jnp.sum(qu * qg, axis=1, keepdims=True))).astype(BF16)

    def f_copy(k):
        other, dev = outer_peer(k)
        send = copy(q_fin.at[rows(o)], q_fin.at[rows(o)], f_ss.at[k], f_rs.at[o], dev)
        recv = copy(q_fin.at[rows(o)], q_fin.at[rows(other)], f_ss.at[k], f_rs.at[other], dev)
        return send, recv

    def f_start(k, _):
        f_copy(k)[0].start()
        return 0

    lax.fori_loop(1, NO, f_start, 0)

    ring_send(2, 1, True)
    ring_send(2, 0, True)
    ring_send(1, 1, True)
    ring_send(1, 0, True)

    other_i, own_i = z * 2 + 1 - xh, z * 2 + xh

    def total(xx, i, h):
        value = mine[i, h * HALF : (h + 1) * HALF, :] + sib_in[
            i, h * HALF : (h + 1) * HALF, :
        ].astype(F32)
        return value + arrived(0, 1, xx, h) + arrived(1, 1, xx, h)

    def x_copy(h):
        part = pl.ds(h * HALF, HALF)
        return copy(x_out.at[part], x_in.at[part], x_ss.at[h], x_rs.at[h], x2)

    sib_copy(other_i).wait_recv()
    sib_copy(own_i).wait_recv()
    for h in range(2):
        x_out[h * HALF : (h + 1) * HALF, :] = total(1 - xh, other_i, h).astype(BF16)
        x_copy(h).start()
    pg_own = [total(xh, own_i, h) for h in range(2)]

    def c_wait(k, _):
        c_copy(k)[1].wait_recv()
        return 0

    def r_wait(k, _):
        r_copy(k)[1].wait_recv()
        return 0

    lax.fori_loop(1, NO, c_wait, 0)
    lax.fori_loop(1, 16, r_wait, 0)
    loss_ref[...] = (jnp.sum(sum_r_all[...], axis=0) + jnp.sum(sum_c_all[...], axis=0)) * (
        LN2 / (2.0 * NB * NP * NO)
    )

    pu = p_ref[...]
    p_inv2 = lax.rsqrt(jnp.sum(pu * pu, axis=1, keepdims=True) + EPS)
    pu = pu * p_inv2

    for h in range(2):
        part = slice(h * HALF, (h + 1) * HALF)
        x_copy(h).wait_recv()
        g = pg_own[h] + x_in[part, :].astype(F32)
        u = pu[part, :]
        po_ref[part, :] = p_inv2[part, :] * (g - u * jnp.sum(u * g, axis=1, keepdims=True))

    def f_wait(k, _):
        f_copy(k)[1].wait_recv()
        return 0

    lax.fori_loop(1, NO, f_wait, 0)

    def ag_done(k, _):
        ag_copy(b, 0, k, sib).wait_send()
        return 0

    def as_done(k, _):
        as_copy(b, k).wait_send()
        return 0

    lax.fori_loop(0, sent[0], ag_done, 0)
    lax.fori_loop(0, sent[1], as_done, 0)
    sib_col.wait_send()
    sib_r.wait_send()
    for h in range(2):
        x_copy(h).wait_send()

    def outer_done(k, _):
        row_copy(k)[0].wait_send()
        c_copy(k)[0].wait_send()
        f_copy(k)[0].wait_send()
        q_copy(outer_peer(k)[0])[0].wait_send()
        return 0

    lax.fori_loop(1, NO, outer_done, 0)

    def chip_done(k, _):
        col_copy(k)[0].wait_send()
        r_copy(k)[0].wait_send()
        return 0

    lax.fori_loop(1, 16, chip_done, 0)

    def sib_done(k, _):
        sib_copy(k).wait_send()
        return 0

    lax.fori_loop(0, 16, sib_done, 0)
    for way in range(2):
        for d in (1, 2, 3, 4):
            for xx in range(2):
                if d < 4 or xx == way:
                    for h in range(2):
                        ring_copy(way, d, xx, h).wait_send()


def widen(q_ref, p_ref, loss_ref, qo_ref, po_ref, lo_ref):
    qo_ref[...] = q_ref[...].astype(F32)
    po_ref[...] = p_ref[...]
    lo_ref[...] = loss_ref[0:1, 0:1]


def per_device(queries, passages, positive_id):
    vmem = pl.BlockSpec(memory_space=pltpu.VMEM)
    hbm = pl.BlockSpec(memory_space=pl.ANY)
    dma = pltpu.SemaphoreType.DMA
    scratch = [
        pltpu.VMEM((NQ, D), F32),
        pltpu.VMEM((NP, D), F32),
        pltpu.VMEM((1, NQ), jnp.int32),
        dma((3,)),
        pltpu.VMEM((NB * NP, D), BF16),
        pltpu.VMEM((NQ, D), BF16),
        pltpu.VMEM((NB * NP, NQ), F32),
        pltpu.VMEM((NB * NP, NQ), BF16),
        pltpu.VMEM((16, NP, D), F32),
        pltpu.VMEM((GROUP, D), F32),
        pltpu.VMEM((16, NP, D), BF16),
        pltpu.VMEM((16, NP, D), BF16),
        pltpu.VMEM((16, NP, D), BF16),
        pltpu.VMEM((16, NP, D), BF16),
        pltpu.VMEM((NP, D), BF16),
        pltpu.VMEM((NP, D), BF16),
        pltpu.VMEM((NO, NP, D), BF16),
        pltpu.VMEM((NO, NP, D), BF16),
        pltpu.VMEM((NP, D), F32),
        pltpu.VMEM((8, NQ), F32),
        pltpu.VMEM((4, 128), F32),
        pltpu.VMEM((1, NQ), F32),
        pltpu.VMEM((NZ, GROUP), F32),
        pltpu.VMEM((NZ, GROUP), F32),
        pltpu.VMEM((NB * NP, 128), F32),
        pltpu.VMEM((16, NZ, GROUP), F32),
        pltpu.VMEM((NO, 8, 128), F32),
        pltpu.VMEM((8, 128), F32),
        pltpu.VMEM((8, 128), F32),
        pltpu.VMEM((16, 8, 128), F32),
        pltpu.VMEM((NO, 8, 128), F32),
        dma((64,)), dma((2 * NB,)), dma((16,)),
        dma((1,)), dma((1,)),
        dma((16,)), dma((16,)),
        dma((NO,)), dma((NO,)),
        dma((16,)), dma((16,)),
        dma((32,)), dma((32,)),
        dma((2,)), dma((2,)),
        dma((NO,)), dma((NO,)),
        dma((NO,)), dma((NO,)),
        dma((1,)), dma((1,)),
        dma((16,)), dma((16,)),
        dma((NO,)), dma((NO,)),
    ]
    qd, pd, loss = pl.pallas_call(
        kernel,
        out_shape=(
            jax.ShapeDtypeStruct((NQ, D), BF16),
            jax.ShapeDtypeStruct((NP, D), F32),
            jax.ShapeDtypeStruct((8, 128), F32),
        ),
        in_specs=[hbm, hbm, hbm],
        out_specs=(vmem, vmem, vmem),
        scratch_shapes=scratch,
        compiler_params=pltpu.CompilerParams(
            collective_id=0, has_side_effects=True, vmem_limit_bytes=56 * 2**20
        ),
    )(queries, passages, positive_id.reshape(1, NQ))
    parts = 2
    return pl.pallas_call(
        widen,
        grid=(parts,),
        out_shape=(
            jax.ShapeDtypeStruct((NQ, D), F32),
            jax.ShapeDtypeStruct((NP, D), F32),
            jax.ShapeDtypeStruct((1, 1), F32),
        ),
        in_specs=[
            pl.BlockSpec((NQ // parts, D), lambda i: (i, 0)),
            pl.BlockSpec((NP // parts, D), lambda i: (i, 0)),
            pl.BlockSpec((8, 128), lambda i: (0, 0)),
        ],
        out_specs=(
            pl.BlockSpec((NQ // parts, D), lambda i: (i, 0)),
            pl.BlockSpec((NP // parts, D), lambda i: (i, 0)),
            pl.BlockSpec((1, 1), lambda i: (0, 0)),
        ),
    )(qd, pd, loss)


def solution(mesh):
    def step(queries, passages, positive_id):
        qd, pd, loss = per_device(queries, passages, positive_id)
        return qd, pd, loss.reshape(())

    placed = (P("blk", None), P(("outer", "blk"), None), P("blk"))
    return jax.shard_map(
        step,
        mesh=mesh,
        in_specs=placed,
        out_specs=(P("blk", None), P(("outer", "blk"), None), P()),
        check_vma=False,
    )
```

time: 102 us -> 87.6 us (0.86)
  Pallas kernels: 95.9 us -> 86.9 us
  local copies, waits for them, and re-layouts: 5.1 us -> 0 us
    pallas_call x1 -> x2, Pallas kernels: 95.9 us -> 86.9 us  [the longest x1 84.3 us: per_device(): pl.pallas_call(kernel, out_shape=(jax.ShapeDtypeStruct((NQ, D), BF16), ja...]
    unnamed x4 -> x0, local copies, waits for them, and re-layouts: 3.91 us -> none
    slice x1 -> x0, local copies, waits for them, and re-layouts: 1.19 us -> none  [per_device(): return (qd, pd, loss[0, 0])]
where the time goes in v3:
time: 87.6 us; the launch traced here: 87.5 us
  Pallas kernels  86.9 us (99%)
    pallas_call x1, Pallas kernels, per_device(): pl.pallas_call(kernel, out_shape=(jax.ShapeDtypeStruct((NQ, D), BF16), ja...  84.3 us
    pallas_call x1, Pallas kernels, per_device(): pl.pallas_call(widen, grid=(parts,), out_shape=(jax.ShapeDtypeStruct((NQ,...  2.56 us

profile of v3, /device:TPU:1, one launch (start us, length us, event | category | flops | bytes accessed | tf_op | source)
XLA Modules:
  0.0 87.5 jit_solution(17039092166366966853)
XLA Ops:
  0.6 84.3 %shard_map.58 = (bf16[512,1024]{1,0:T(8,128)(2,1)}, f32[64,1024]{1,0:T(8,128)}, f32[8,128]{1,0:T(8,128)}) custom-call(f32[512,1024]{1,0:T(8,128)} %q_any.1, f32[64,1024]{1,0:T(8,128)} %p_any.1, s32[1,512]{1,0:T(1,128)} %bitcast.2), custom_call_target="tpu_custom_call" | custom-call | tf_op jit(solution)/shard_map/pallas_call | solution.py:580
  84.9 2.6 %shard_map.59 = (f32[512,1024]{1,0:T(8,128)}, f32[64,1024]{1,0:T(8,128)}, f32[1,1]{1,0:T(1,128)}) custom-call(bf16[512,1024]{1,0:T(8,128)(2,1)} %get-tuple-element.9.q_ref, f32[64,1024]{1,0:T(8,128)} %get-tuple-element.10.p_ref, f32[8,128]{1,0:T(8,128)} %get-tuple-element.11.loss_ref), custom_call_target="tpu_custom_call" | custom-call | tf_op jit(solution)/shard_map/pallas_call | solution.py:595

commit v4 on v3

--- a/solution.py
+++ b/solution.py
@@ -11,7 +11,10 @@
 LN2 = 0.6931471805599453
 SHARP2 = SHARP / LN2
 HALF = 32
-CROSS = (0,)
+CROSS = (0, 1)
+ORDER = (
+    ((0, 1), (1, 0)), ((1, 1), (2, 0)), ((2, 1),), ((3, 0),), ((3, 1),), (), ((4, 0), (4, 1)), (),
+)
 D = 1024
 NQ = 512
 NP = 64
@@ -40,7 +43,7 @@
     q_fin, po_ref, loss_ref,
     q_ref, p_ref, id_ref, in_sem,
     pall, qh, scores, weights, mine, pres, sib_out, sib_in, ring_out, ring_in,
-    x_out, x_in, q_out, q_in, q_own,
+    x_out, x_in, q_out, q_in, q_own, q_done_rows, own_sem,
     row_part, row_wide, pos_acc, col_part, col_sib, col_wide, col_all, row_all,
     sum_r, sum_r_sib, sum_r_all, sum_c_all,
     ag_ss, ag_rs, as_ss, cs_ss, cs_rs, col_ss, col_rs, row_ss, row_rs,
@@ -60,8 +63,14 @@
     def wrap(dz):
         return lax.rem(z + dz + 16, NZ)
 
+    y = lax.rem(o, 4)
+    xl = lax.div(o, 4)
+
+    def outer_of(xx):
+        return lax.rem(xl + xx + xh, 2) * 4 + y
+
     def at(zz, xx, cc):
-        return (blk_of(zz, xx, cc), o)
+        return (blk_of(zz, xx, cc), outer_of(xx))
 
     sib = at(z, xh, 1 - c)
     x2 = at(z, 1 - xh, c)
@@ -70,7 +79,7 @@
 
     def chip_peer(k):
         other = lax.rem(chip + k, 16)
-        return other, (other * 2 + c, o)
+        return other, (other * 2 + c, outer_of(lax.rem(other, 2)))
 
     def outer_peer(k):
         other = lax.rem(o + k, NO)
@@ -175,37 +184,17 @@
             as_copy(blk_of(wrap(dz), xx, 1 - c), 0).wait_recv()
 
     def gather_turn(t):
-        if t == 0:
-            got(0, 1)
-            got(1, 0)
-            from_sib(0)
-        if t == 1:
-            got(1, 1)
-            got(2, 0)
-            from_sib(-1)
-        if t == 2:
-            got(2, 1)
-            from_sib(1)
-        if t == 3:
-            got(3, 0)
-            from_sib(-2)
-        if t == 4:
-            got(3, 1)
-            from_sib(2)
-        if t == 5:
-            from_sib(-3)
-        if t == 6:
-            got(4, 0)
-            got(4, 1)
-            from_sib(3)
-        if t == 7:
-            from_sib(4)
-
-    base = o * (NB * NP)
+        for k, step in enumerate(ORDER):
+            if t == k:
+                for dz, xrel in step:
+                    got(dz, xrel)
+        from_sib((0, -1, 1, -2, 2, -3, 3, 4)[t])
+
+    base = [outer_of(xx) * (NB * NP) for xx in range(2)]
 
     def mask_of(zz):
-        cols = base + zz * GROUP + lax.broadcasted_iota(jnp.int32, (GROUP, NQ), 0)
-        return cols == id_ref[...]
+        row = lax.broadcasted_iota(jnp.int32, (GROUP, NQ), 0)
+        return row + zz * GROUP + jnp.where(row < GROUP // 2, base[0], base[1]) == id_ref[...]
 
     def first(t, _):
         for k in range(8):
@@ -267,7 +256,8 @@
     rall = row_all[...]
     row_lse4 = lse_of(rall[:, 0:4, :], 0)[0]
     pos4 = jnp.sum(rall[:, 4:8, :], axis=0)
-    row_wide[...] = row_lse4 + 1.0
+    for k in range(4):
+        row_wide[:, 128 * k : 128 * k + 128] = row_lse4[k : k + 1, :] + 1.0
     sum_r[...] = jnp.broadcast_to(jnp.sum(row_lse4 - 2.0 * pos4, keepdims=True), (8, 128))
     sib_r = copy(sum_r, sum_r_sib, r1_ss.at[0], r1_rs.at[0], sib)
     sib_r.start()
@@ -282,51 +272,47 @@
         col_wide[k * GROUP : (k + 1) * GROUP, :] = jnp.broadcast_to(
             col_lse[k : k + 1, :] + 1.0, (128, GROUP)
         ).T
-    sum_c_all[o] = jnp.broadcast_to(jnp.sum(col_lse, keepdims=True), (8, 128))
+    def passage_set(oo):
+        return lax.rem(lax.div(oo, 4) + xh, 2) * 4 + lax.rem(oo, 4)
+
+    sum_c_all[passage_set(o)] = jnp.broadcast_to(jnp.sum(col_lse, keepdims=True), (8, 128))
 
     def c_copy(k):
         other, dev = outer_peer(k)
-        send = copy(sum_c_all.at[o], sum_c_all.at[o], ca_ss.at[k], ca_rs.at[o], dev)
-        recv = copy(sum_c_all.at[o], sum_c_all.at[other], ca_ss.at[k], ca_rs.at[other], dev)
+        me, it = passage_set(o), passage_set(other)
+        send = copy(sum_c_all.at[me], sum_c_all.at[me], ca_ss.at[k], ca_rs.at[me], dev)
+        recv = copy(sum_c_all.at[me], sum_c_all.at[it], ca_ss.at[k], ca_rs.at[it], dev)
         return send, recv
 
-    def q_copy(other):
+    def tile(g, _):
+        s = scores[rows(g, GROUP), :]
+        cl = col_wide[rows(g, GROUP), :]
+        w = jnp.exp2(s - row_wide[...]) + jnp.exp2(s - jnp.concatenate([cl] * 4, axis=1))
+        weights[rows(g, GROUP), :] = (w - jnp.where(mask_of(g), 1.0, 0.0)).astype(BF16)
+        return 0
+
+    lax.fori_loop(0, NZ, tile, 0)
+
+    def q_copy(st, other):
         dev = (b, other)
-        send = copy(q_out.at[other], q_in.at[o], q_ss.at[other], q_rs.at[o], dev)
-        recv = copy(q_out.at[other], q_in.at[other], q_ss.at[other], q_rs.at[other], dev)
+        i, mine_i = st * NO + other, st * NO + o
+        send = copy(q_out.at[i], q_in.at[mine_i], q_ss.at[i], q_rs.at[mine_i], dev)
+        recv = copy(q_out.at[i], q_in.at[i], q_ss.at[i], q_rs.at[i], dev)
         return send, recv
 
-    def q_chunk(k, _):
-        k = lax.rem(k + lax.div(o, 2), 4)
-        lanes = pl.ds(pl.multiple_of(k * 128, 128), 128)
-        rl = row_wide[pl.ds(k, 1), :]
-        ids = id_ref[:, lanes] - base
-
-        def tile(g, _):
-            s = scores[rows(g, GROUP), lanes]
-            cols = g * GROUP + lax.broadcasted_iota(jnp.int32, (GROUP, 128), 0)
-            w = jnp.exp2(s - rl) + jnp.exp2(s - col_wide[rows(g, GROUP), :])
-            weights[rows(g, GROUP), lanes] = (w - jnp.where(cols == ids, 1.0, 0.0)).astype(BF16)
-            return 0
-
-        lax.fori_loop(0, NZ, tile, 0)
-        g = dot(weights[:, lanes], pall[...], TN)
-        for h in range(2):
-            other = 2 * k + h
-            part = g[h * NP : (h + 1) * NP, :]
+    def q_stage(st):
+        g = dot(weights[:, st * 256 : (st + 1) * 256], pall[...], TN)
+        for other in range(NO):
+            part = g[other * HALF : (other + 1) * HALF, :]
 
             @pl.when(other == o)
             def _():
-                q_own[...] = part
+                q_own[st] = part
 
             @pl.when(other != o)
             def _():
-                q_out[other] = part.astype(BF16)
-                q_copy(other)[0].start()
-
-        return 0
-
-    lax.fori_loop(0, 4, q_chunk, 0)
+                q_out[st * NO + other] = part.astype(BF16)
+                q_copy(st, other)[0].start()
 
     def sib_copy(i):
         return copy(sib_out.at[i], sib_in.at[i], sib_ss.at[i], sib_rs.at[i], sib)
@@ -363,6 +349,7 @@
                 ring_copy(way, d, xx, h).start()
 
     def second(t, _):
+        pl.when(t == 3)(lambda: q_stage(0))
         far_by = 4 - lax.div(t + 1, 2)
         zz = wrap(jnp.where(lax.rem(t, 2) == 1, far_by, -far_by))
         pres[...] = SHARP * dot(weights[rows(zz, GROUP), :], qh[...], NN)
@@ -376,13 +363,14 @@
         return 0
 
     lax.fori_loop(0, 8, second, 0)
+    q_stage(1)
+    ring_send(3, 0, True)
 
     def c_start(k, _):
         c_copy(k)[0].start()
         return 0
 
     lax.fori_loop(1, NO, c_start, 0)
-    ring_send(3, 0, True)
     sib_r.wait_recv()
     sum_r_all[chip] = sum_r[...] + sum_r_sib[...]
 
@@ -398,35 +386,88 @@
 
     lax.fori_loop(1, 16, r_start, 0)
 
-    def q_add(k, _):
-        other, _dev = outer_peer(k)
-        q_copy(other)[1].wait_recv()
-        q_own[...] += q_in[other].astype(F32)
-        return 0
-
-    lax.fori_loop(1, NO, q_add, 0)
-    qv = q_ref[rows(o), :]
-    q_inv = lax.rsqrt(jnp.sum(qv * qv, axis=1, keepdims=True) + EPS)
-    qu = qv * q_inv
-    qg = SHARP * q_own[...]
-    q_fin[rows(o), :] = (q_inv * (qg - qu * jnp.sum(qu * qg, axis=1, keepdims=True))).astype(BF16)
-
-    def f_copy(k):
-        other, dev = outer_peer(k)
-        send = copy(q_fin.at[rows(o)], q_fin.at[rows(o)], f_ss.at[k], f_rs.at[o], dev)
-        recv = copy(q_fin.at[rows(o)], q_fin.at[rows(other)], f_ss.at[k], f_rs.at[other], dev)
-        return send, recv
-
-    def f_start(k, _):
-        f_copy(k)[0].start()
-        return 0
-
-    lax.fori_loop(1, NO, f_start, 0)
-
+    def ag_done(k, _):
+        ag_copy(b, 0, k, sib).wait_send()
+        return 0
+
+    def as_done(k, _):
+        as_copy(b, k).wait_send()
+        return 0
+
+    def row_done(k, _):
+        row_copy(k)[0].wait_send()
+        return 0
+
+    def col_done(k, _):
+        col_copy(k)[0].wait_send()
+        return 0
+
+    lax.fori_loop(0, sent[0], ag_done, 0)
+    lax.fori_loop(0, sent[1], as_done, 0)
+    lax.fori_loop(1, NO, row_done, 0)
+    lax.fori_loop(1, 16, col_done, 0)
+    sib_col.wait_send()
+    sib_r.wait_send()
     ring_send(2, 1, True)
     ring_send(2, 0, True)
+
+    def sib_done(k, _):
+        sib_copy(k).wait_send()
+        return 0
+
+    lax.fori_loop(0, 16, sib_done, 0)
+
+    def q_rows(st, other):
+        return pl.ds(pl.multiple_of(st * 256 + other * HALF, HALF), HALF)
+
+    def f_copy(st, k):
+        other, dev = outer_peer(k)
+        here, there = q_fin.at[q_rows(st, o)], q_fin.at[q_rows(st, other)]
+        send = copy(q_done_rows.at[st], here, f_ss.at[st * NO + k], f_rs.at[st * NO + o], dev)
+        recv = copy(q_done_rows.at[st], there, f_ss.at[st * NO + k], f_rs.at[st * NO + other], dev)
+        return send, recv
+
+    def f_own(st):
+        return pltpu.make_async_copy(q_done_rows.at[st], q_fin.at[q_rows(st, o)], own_sem.at[st])
+
+    def q_finish(st):
+        def q_add(k, _):
+            other, _dev = outer_peer(k)
+            q_copy(st, other)[1].wait_recv()
+            q_own[st] += q_in[st * NO + other].astype(F32)
+            return 0
+
+        lax.fori_loop(1, NO, q_add, 0)
+        qv = q_ref[q_rows(st, o), :]
+        q_inv = lax.rsqrt(jnp.sum(qv * qv, axis=1, keepdims=True) + EPS)
+        qu = qv * q_inv
+        qg = SHARP * q_own[st]
+        q_done_rows[st] = (
+            q_inv * (qg - qu * jnp.sum(qu * qg, axis=1, keepdims=True))
+        ).astype(BF16)
+
+        def f_start(k, _):
+            f_copy(st, k)[0].start()
+            return 0
+
+        lax.fori_loop(1, NO, f_start, 0)
+        f_own(st).start()
+
+    q_finish(0)
     ring_send(1, 1, True)
     ring_send(1, 0, True)
+    for way in range(2):
+        for d, xx in ((4, way), (3, 0), (3, 1)):
+            for h in range(2):
+                ring_copy(way, d, xx, h).wait_send()
+    q_finish(1)
+
+    def q_done(k, _):
+        for st in range(2):
+            q_copy(st, outer_peer(k)[0])[0].wait_send()
+        return 0
+
+    lax.fori_loop(1, NO, q_done, 0)
 
     other_i, own_i = z * 2 + 1 - xh, z * 2 + xh
 
@@ -473,53 +514,35 @@
         po_ref[part, :] = p_inv2[part, :] * (g - u * jnp.sum(u * g, axis=1, keepdims=True))
 
     def f_wait(k, _):
-        f_copy(k)[1].wait_recv()
+        f_copy(0, k)[1].wait_recv()
+        f_copy(1, k)[1].wait_recv()
         return 0
 
     lax.fori_loop(1, NO, f_wait, 0)
 
-    def ag_done(k, _):
-        ag_copy(b, 0, k, sib).wait_send()
-        return 0
-
-    def as_done(k, _):
-        as_copy(b, k).wait_send()
-        return 0
-
-    lax.fori_loop(0, sent[0], ag_done, 0)
-    lax.fori_loop(0, sent[1], as_done, 0)
-    sib_col.wait_send()
-    sib_r.wait_send()
     for h in range(2):
         x_copy(h).wait_send()
 
     def outer_done(k, _):
-        row_copy(k)[0].wait_send()
         c_copy(k)[0].wait_send()
-        f_copy(k)[0].wait_send()
-        q_copy(outer_peer(k)[0])[0].wait_send()
+        for st in range(2):
+            f_copy(st, k)[0].wait_send()
         return 0
 
     lax.fori_loop(1, NO, outer_done, 0)
 
     def chip_done(k, _):
-        col_copy(k)[0].wait_send()
         r_copy(k)[0].wait_send()
         return 0
 
     lax.fori_loop(1, 16, chip_done, 0)
-
-    def sib_done(k, _):
-        sib_copy(k).wait_send()
-        return 0
-
-    lax.fori_loop(0, 16, sib_done, 0)
     for way in range(2):
-        for d in (1, 2, 3, 4):
+        for d in (1, 2):
             for xx in range(2):
-                if d < 4 or xx == way:
-                    for h in range(2):
-                        ring_copy(way, d, xx, h).wait_send()
+                for h in range(2):
+                    ring_copy(way, d, xx, h).wait_send()
+    for st in range(2):
+        f_own(st).wait()
 
 
 def widen(q_ref, p_ref, loss_ref, qo_ref, po_ref, lo_ref):
@@ -549,11 +572,13 @@
         pltpu.VMEM((16, NP, D), BF16),
         pltpu.VMEM((NP, D), BF16),
         pltpu.VMEM((NP, D), BF16),
-        pltpu.VMEM((NO, NP, D), BF16),
-        pltpu.VMEM((NO, NP, D), BF16),
-        pltpu.VMEM((NP, D), F32),
+        pltpu.VMEM((2 * NO, HALF, D), BF16),
+        pltpu.VMEM((2 * NO, HALF, D), BF16),
+        pltpu.VMEM((2, HALF, D), F32),
+        pltpu.VMEM((2, HALF, D), BF16),
+        dma((2,)),
         pltpu.VMEM((8, NQ), F32),
-        pltpu.VMEM((4, 128), F32),
+        pltpu.VMEM((1, NQ), F32),
         pltpu.VMEM((1, NQ), F32),
         pltpu.VMEM((NZ, GROUP), F32),
         pltpu.VMEM((NZ, GROUP), F32),
@@ -571,8 +596,8 @@
         dma((16,)), dma((16,)),
         dma((32,)), dma((32,)),
         dma((2,)), dma((2,)),
-        dma((NO,)), dma((NO,)),
-        dma((NO,)), dma((NO,)),
+        dma((2 * NO,)), dma((2 * NO,)),
+        dma((2 * NO,)), dma((2 * NO,)),
         dma((1,)), dma((1,)),
         dma((16,)), dma((16,)),
         dma((NO,)), dma((NO,)),
@@ -585,7 +610,7 @@
             jax.ShapeDtypeStruct((8, 128), F32),
         ),
         in_specs=[hbm, hbm, hbm],
-        out_specs=(vmem, vmem, vmem),
+        out_specs=(hbm, vmem, vmem),
         scratch_shapes=scratch,
         compiler_params=pltpu.CompilerParams(
             collective_id=0, has_side_effects=True, vmem_limit_bytes=56 * 2**20

time: 87.6 us -> 85.3 us (0.974)
  Pallas kernels: 86.9 us -> 84.5 us
    pallas_call x1, Pallas kernels: 84.3 us -> 82 us  [per_device(): pl.pallas_call(kernel, out_shape=(jax.ShapeDtypeStruct((NQ, D), BF16), ja...]
where the time goes in v4:
time: 85.3 us; the launch traced here: 85.2 us
  Pallas kernels  84.5 us (99%)
    pallas_call x1, Pallas kernels, per_device(): pl.pallas_call(kernel, out_shape=(jax.ShapeDtypeStruct((NQ, D), BF16), ja...  82 us
    pallas_call x1, Pallas kernels, per_device(): pl.pallas_call(widen, grid=(parts,), out_shape=(jax.ShapeDtypeStruct((NQ,...  2.56 us

profile of v4, /device:TPU:1, one launch (start us, length us, event | category | flops | bytes accessed | tf_op | source)
XLA Modules:
  0.0 85.2 jit_solution(6810109547306514103)
XLA Ops:
  0.6 82.0 %shard_map.58 = (bf16[512,1024]{1,0:T(8,128)(2,1)}, f32[64,1024]{1,0:T(8,128)}, f32[8,128]{1,0:T(8,128)}) custom-call(f32[512,1024]{1,0:T(8,128)} %q_any.1, f32[64,1024]{1,0:T(8,128)} %p_any.1, s32[1,512]{1,0:T(1,128)} %bitcast.2), custom_call_target="tpu_custom_call" | custom-call | tf_op jit(solution)/shard_map/pallas_call | solution.py:605
  82.6 2.6 %shard_map.59 = (f32[512,1024]{1,0:T(8,128)}, f32[64,1024]{1,0:T(8,128)}, f32[1,1]{1,0:T(1,128)}) custom-call(bf16[512,1024]{1,0:T(8,128)(2,1)} %get-tuple-element.9.q_ref, f32[64,1024]{1,0:T(8,128)} %get-tuple-element.10.p_ref, f32[8,128]{1,0:T(8,128)} %get-tuple-element.11.loss_ref), custom_call_target="tpu_custom_call" | custom-call | tf_op jit(solution)/shard_map/pallas_call | solution.py:620

commit v5 on v4

--- a/solution.py
+++ b/solution.py
@@ -243,7 +243,8 @@
         return send, recv
 
     def col_start(k, _):
-        col_copy(k)[0].start()
+        by = lax.div(k, 2)
+        col_copy(8 + jnp.where(lax.rem(k, 2) == 0, by, -by))[0].start()
         return 0
 
     lax.fori_loop(1, 16, col_start, 0)
@@ -284,14 +285,20 @@
         recv = copy(sum_c_all.at[me], sum_c_all.at[it], ca_ss.at[k], ca_rs.at[it], dev)
         return send, recv
 
-    def tile(g, _):
+    def far(t):
+        by = 4 - lax.div(t + 1, 2)
+        return wrap(jnp.where(lax.rem(t, 2) == 1, by, -by))
+
+    def weights_of(t):
+        g = far(t)
         s = scores[rows(g, GROUP), :]
         cl = col_wide[rows(g, GROUP), :]
         w = jnp.exp2(s - row_wide[...]) + jnp.exp2(s - jnp.concatenate([cl] * 4, axis=1))
         weights[rows(g, GROUP), :] = (w - jnp.where(mask_of(g), 1.0, 0.0)).astype(BF16)
-        return 0
-
-    lax.fori_loop(0, NZ, tile, 0)
+
+    def tile(t, _):
+        weights_of(t)
+        return 0
 
     def q_copy(st, other):
         dev = (b, other)
@@ -348,10 +355,37 @@
                 ring_out[slot(way, d, xx), h * HALF : (h + 1) * HALF, :] = value.astype(BF16)
                 ring_copy(way, d, xx, h).start()
 
+    def last_copy(way, rel, h):
+        i = slot(way, 1, rel)
+        part = pl.ds(h * HALF, HALF)
+        to = at(wrap(1 if way == 0 else -1), xh if rel == 0 else 1 - xh, c)
+        return copy(
+            ring_out.at[i, part], ring_in.at[i, part],
+            ring_ss.at[i * 2 + h], ring_rs.at[i * 2 + h], to,
+        )
+
+    def last_send(rel):
+        xx = xh if rel == 0 else 1 - xh
+        for h in range(2):
+            part = slice(h * HALF, (h + 1) * HALF)
+            for way in range(2):
+                value = joined(1 if way == 0 else -1, xx, h) + arrived(way, 2, xx, h)
+                ring_out[slot(way, 1, rel), part, :] = value.astype(BF16)
+                last_copy(way, rel, h).start()
+
+    def x_copy(h):
+        part = pl.ds(h * HALF, HALF)
+        return copy(x_out.at[part], x_in.at[part], x_ss.at[h], x_rs.at[h], x2)
+
     def second(t, _):
-        pl.when(t == 3)(lambda: q_stage(0))
-        far_by = 4 - lax.div(t + 1, 2)
-        zz = wrap(jnp.where(lax.rem(t, 2) == 1, far_by, -far_by))
+        pl.when(t < 2)(lambda: weights_of(t))
+
+        @pl.when(t == 2)
+        def _():
+            lax.fori_loop(2, NZ, tile, 0)
+            q_stage(0)
+
+        zz = far(t)
         pres[...] = SHARP * dot(weights[rows(zz, GROUP), :], qh[...], NN)
         for xx in range(2):
             i = zz * 2 + xx
@@ -365,6 +399,9 @@
     lax.fori_loop(0, 8, second, 0)
     q_stage(1)
     ring_send(3, 0, True)
+    for h in range(2):
+        x_out[h * HALF : (h + 1) * HALF, :] = joined(0, 1 - xh, h).astype(BF16)
+        x_copy(h).start()
 
     def c_start(k, _):
         c_copy(k)[0].start()
@@ -454,8 +491,8 @@
         f_own(st).start()
 
     q_finish(0)
-    ring_send(1, 1, True)
-    ring_send(1, 0, True)
+    last_send(1)
+    last_send(0)
     for way in range(2):
         for d, xx in ((4, way), (3, 0), (3, 1)):
             for h in range(2):
@@ -469,24 +506,11 @@
 
     lax.fori_loop(1, NO, q_done, 0)
 
-    other_i, own_i = z * 2 + 1 - xh, z * 2 + xh
-
-    def total(xx, i, h):
-        value = mine[i, h * HALF : (h + 1) * HALF, :] + sib_in[
-            i, h * HALF : (h + 1) * HALF, :
-        ].astype(F32)
-        return value + arrived(0, 1, xx, h) + arrived(1, 1, xx, h)
-
-    def x_copy(h):
-        part = pl.ds(h * HALF, HALF)
-        return copy(x_out.at[part], x_in.at[part], x_ss.at[h], x_rs.at[h], x2)
-
-    sib_copy(other_i).wait_recv()
-    sib_copy(own_i).wait_recv()
-    for h in range(2):
-        x_out[h * HALF : (h + 1) * HALF, :] = total(1 - xh, other_i, h).astype(BF16)
-        x_copy(h).start()
-    pg_own = [total(xh, own_i, h) for h in range(2)]
+    own_i = z * 2 + xh
+
+    def last_arrived(way, rel, h):
+        last_copy(way, rel, h).wait_recv()
+        return ring_in[slot(way, 1, rel), h * HALF : (h + 1) * HALF, :].astype(F32)
 
     def c_wait(k, _):
         c_copy(k)[1].wait_recv()
@@ -509,7 +533,9 @@
     for h in range(2):
         part = slice(h * HALF, (h + 1) * HALF)
         x_copy(h).wait_recv()
-        g = pg_own[h] + x_in[part, :].astype(F32)
+        g = joined(0, xh, h) + x_in[part, :].astype(F32)
+        for rel in (1, 0):
+            g = g + last_arrived(0, rel, h) + last_arrived(1, rel, h)
         u = pu[part, :]
         po_ref[part, :] = p_inv2[part, :] * (g - u * jnp.sum(u * g, axis=1, keepdims=True))
 

time: 85.3 us -> 83.1 us (0.974)
  Pallas kernels: 84.5 us -> 82.3 us
    pallas_call x1, Pallas kernels: 82 us -> 79.7 us  [per_device(): pl.pallas_call(kernel, out_shape=(jax.ShapeDtypeStruct((NQ, D), BF16), ja...]
where the time goes in v5:
time: 83.1 us; the launch traced here: 82.9 us
  Pallas kernels  82.3 us (99%)
    pallas_call x1, Pallas kernels, per_device(): pl.pallas_call(kernel, out_shape=(jax.ShapeDtypeStruct((NQ, D), BF16), ja...  79.7 us
    pallas_call x1, Pallas kernels, per_device(): pl.pallas_call(widen, grid=(parts,), out_shape=(jax.ShapeDtypeStruct((NQ,...  2.56 us

profile of v5, /device:TPU:1, one launch (start us, length us, event | category | flops | bytes accessed | tf_op | source)
XLA Modules:
  0.0 82.9 jit_solution(10181384383428506892)
XLA Ops:
  0.6 79.7 %shard_map.58 = (bf16[512,1024]{1,0:T(8,128)(2,1)}, f32[64,1024]{1,0:T(8,128)}, f32[8,128]{1,0:T(8,128)}) custom-call(f32[512,1024]{1,0:T(8,128)} %q_any.1, f32[64,1024]{1,0:T(8,128)} %p_any.1, s32[1,512]{1,0:T(1,128)} %bitcast.2), custom_call_target="tpu_custom_call" | custom-call | tf_op jit(solution)/shard_map/pallas_call | solution.py:631
  80.4 2.6 %shard_map.59 = (f32[512,1024]{1,0:T(8,128)}, f32[64,1024]{1,0:T(8,128)}, f32[1,1]{1,0:T(1,128)}) custom-call(bf16[512,1024]{1,0:T(8,128)(2,1)} %get-tuple-element.9.q_ref, f32[64,1024]{1,0:T(8,128)} %get-tuple-element.10.p_ref, f32[8,128]{1,0:T(8,128)} %get-tuple-element.11.loss_ref), custom_call_target="tpu_custom_call" | custom-call | tf_op jit(solution)/shard_map/pallas_call | solution.py:646

commit v6 on v5

--- a/solution.py
+++ b/solution.py
@@ -11,9 +11,9 @@
 LN2 = 0.6931471805599453
 SHARP2 = SHARP / LN2
 HALF = 32
-CROSS = (0, 1)
+CROSS = (0,)
 ORDER = (
-    ((0, 1), (1, 0)), ((1, 1), (2, 0)), ((2, 1),), ((3, 0),), ((3, 1),), (), ((4, 0), (4, 1)), (),
+    ((1, 0), (1, 1), (0, 1)), ((2, 0), (2, 1)), (), ((3, 0), (3, 1)), (), (), ((4, 0), (4, 1)), (),
 )
 D = 1024
 NQ = 512
@@ -76,6 +76,8 @@
     x2 = at(z, 1 - xh, c)
     up = at(wrap(1), xh, c)
     down = at(wrap(-1), xh, c)
+    x2_up = at(wrap(1), 1 - xh, c)
+    x2_down = at(wrap(-1), 1 - xh, c)
 
     def chip_peer(k):
         other = lax.rem(chip + k, 16)
@@ -95,7 +97,7 @@
     id_load = pltpu.make_async_copy(id_any, id_ref, in_sem.at[2])
     p_load.start()
     barrier = pltpu.get_barrier_semaphore()
-    for dev in (x2, up, down, sib):
+    for dev in (x2, up, down, x2_up, x2_down, sib):
         pl.semaphore_signal(barrier, inc=1, device_id=dev, device_id_type=MESH)
 
     def greet_outer(k, _):
@@ -116,7 +118,7 @@
     pv = p_ref[...]
     p_inv = lax.rsqrt(jnp.sum(pv * pv, axis=1, keepdims=True) + EPS)
     pall[rows(b), :] = (pv * p_inv).astype(BF16)
-    pl.semaphore_wait(barrier, 4 + NO - 1)
+    pl.semaphore_wait(barrier, 6 + NO - 1)
 
     def piece(i, h):
         return pall.at[pl.ds(pl.multiple_of(i * NP + h * HALF, HALF), HALF)]
@@ -139,7 +141,9 @@
         sent[1] += 1
 
     for h in range(2):
-        pass_on(b, h, up, down, x2)
+        pass_on(b, h, up, down, x2_up, x2_down)
+    for h in range(2):
+        pass_on(b, h, x2)
     to_sib(b)
 
     def norm_q(i, _):
@@ -166,7 +170,7 @@
                 ag_copy(i, h, 0, sib).wait_recv()
                 if xrel == 0 and dz in CROSS and dz > 0:
                     pass_on(i, h, x2)
-                if dz < 3 and (xrel == 0 or dz + 1 not in CROSS):
+                if 0 < dz < 3 and (xrel == 0 or dz + 1 not in CROSS):
                     if d <= 0:
                         pass_on(i, h, up)
                     if d >= 0:

time: 83.1 us -> 82 us (0.987)
  Pallas kernels: 82.3 us -> 81.3 us
    pallas_call x1, Pallas kernels: 79.7 us -> 78.7 us  [per_device(): pl.pallas_call(kernel, out_shape=(jax.ShapeDtypeStruct((NQ, D), BF16), ja...]
where the time goes in v6:
time: 82 us; the launch traced here: 81.9 us
  Pallas kernels  81.3 us (99%)
    pallas_call x1, Pallas kernels, per_device(): pl.pallas_call(kernel, out_shape=(jax.ShapeDtypeStruct((NQ, D), BF16), ja...  78.7 us
    pallas_call x1, Pallas kernels, per_device(): pl.pallas_call(widen, grid=(parts,), out_shape=(jax.ShapeDtypeStruct((NQ,...  2.56 us

profile of v6, /device:TPU:1, one launch (start us, length us, event | category | flops | bytes accessed | tf_op | source)
XLA Modules:
  0.0 81.9 jit_solution(2077831017578210406)
XLA Ops:
  0.6 78.7 %shard_map.58 = (bf16[512,1024]{1,0:T(8,128)(2,1)}, f32[64,1024]{1,0:T(8,128)}, f32[8,128]{1,0:T(8,128)}) custom-call(f32[512,1024]{1,0:T(8,128)} %q_any.1, f32[64,1024]{1,0:T(8,128)} %p_any.1, s32[1,512]{1,0:T(1,128)} %bitcast.2), custom_call_target="tpu_custom_call" | custom-call | tf_op jit(solution)/shard_map/pallas_call | solution.py:635
  79.4 2.6 %shard_map.59 = (f32[512,1024]{1,0:T(8,128)}, f32[64,1024]{1,0:T(8,128)}, f32[1,1]{1,0:T(1,128)}) custom-call(bf16[512,1024]{1,0:T(8,128)(2,1)} %get-tuple-element.9.q_ref, f32[64,1024]{1,0:T(8,128)} %get-tuple-element.10.p_ref, f32[8,128]{1,0:T(8,128)} %get-tuple-element.11.loss_ref), custom_call_target="tpu_custom_call" | custom-call | tf_op jit(solution)/shard_map/pallas_call | solution.py:650

commit v7 on v6

--- a/solution.py
+++ b/solution.py
@@ -313,17 +313,16 @@
 
     def q_stage(st):
         g = dot(weights[:, st * 256 : (st + 1) * 256], pall[...], TN)
-        for other in range(NO):
-            part = g[other * HALF : (other + 1) * HALF, :]
-
-            @pl.when(other == o)
-            def _():
-                q_own[st] = part
-
-            @pl.when(other != o)
-            def _():
-                q_out[st * NO + other] = part.astype(BF16)
-                q_copy(st, other)[0].start()
+        pres[...] = g
+
+        def q_send(k, _):
+            other, _dev = outer_peer(k)
+            q_out[st * NO + other] = pres[rows(other, HALF), :].astype(BF16)
+            q_copy(st, other)[0].start()
+            return 0
+
+        lax.fori_loop(1, NO, q_send, 0)
+        q_own[st] = pres[rows(o, HALF), :]
 
     def sib_copy(i):
         return copy(sib_out.at[i], sib_in.at[i], sib_ss.at[i], sib_rs.at[i], sib)

time: 82 us -> 80.9 us (0.987)
  Pallas kernels: 81.3 us -> 80 us
    pallas_call x1, Pallas kernels: 78.7 us -> 77.5 us  [per_device(): pl.pallas_call(kernel, out_shape=(jax.ShapeDtypeStruct((NQ, D), BF16), ja...]
where the time goes in v7:
time: 80.9 us; the launch traced here: 80.7 us
  Pallas kernels  80 us (99%)
    pallas_call x1, Pallas kernels, per_device(): pl.pallas_call(kernel, out_shape=(jax.ShapeDtypeStruct((NQ, D), BF16), ja...  77.5 us
    pallas_call x1, Pallas kernels, per_device(): pl.pallas_call(widen, grid=(parts,), out_shape=(jax.ShapeDtypeStruct((NQ,...  2.56 us

profile of v7, /device:TPU:1, one launch (start us, length us, event | category | flops | bytes accessed | tf_op | source)
XLA Modules:
  0.0 80.7 jit_solution(3880792716951241048)
XLA Ops:
  0.6 77.5 %shard_map.58 = (bf16[512,1024]{1,0:T(8,128)(2,1)}, f32[64,1024]{1,0:T(8,128)}, f32[8,128]{1,0:T(8,128)}) custom-call(f32[512,1024]{1,0:T(8,128)} %q_any.1, f32[64,1024]{1,0:T(8,128)} %p_any.1, s32[1,512]{1,0:T(1,128)} %bitcast.2), custom_call_target="tpu_custom_call" | custom-call | tf_op jit(solution)/shard_map/pallas_call | solution.py:634
  78.1 2.6 %shard_map.59 = (f32[512,1024]{1,0:T(8,128)}, f32[64,1024]{1,0:T(8,128)}, f32[1,1]{1,0:T(1,128)}) custom-call(bf16[512,1024]{1,0:T(8,128)(2,1)} %get-tuple-element.9.q_ref, f32[64,1024]{1,0:T(8,128)} %get-tuple-element.10.p_ref, f32[8,128]{1,0:T(8,128)} %get-tuple-element.11.loss_ref), custom_call_target="tpu_custom_call" | custom-call | tf_op jit(solution)/shard_map/pallas_call | solution.py:649
